TPU v7x, 128 devices: a whole 4x4x4 slice. The times are simulated.
128 devices in a mesh: band: 8 (over y, core), tile: 16 (over x, z).
Axes of the slice: x: 4, y: 4, z: 4, core: 2. Of those that a mesh axis runs over, the one named last changes fastest.
Arguments:
- wind_east: float32 [16, 1024, 1024], P(None, 'tile', 'band'), may hold values from -2.5 to 2.5
- wind_north: float32 [16, 1024, 1024], P(None, 'tile', 'band'), may hold values from -2.5 to 2.5
- theta_pert: float32 [16, 1024, 1024], P(None, 'tile', 'band'), may hold values from -6 to 6
- tke_field: float32 [16, 1024, 1024], P(None, 'tile', 'band'), may hold values from 0.1 to 1
- target_east: float32 [16, 1024, 1024], P(None, 'tile', 'band'), may hold values from -2.5 to 2.5
- target_north: float32 [16, 1024, 1024], P(None, 'tile', 'band'), may hold values from -2.5 to 2.5
- target_theta: float32 [16, 1024, 1024], P(None, 'tile', 'band'), may hold values from -6 to 6
- turbine_count: int32 [1024, 1024], P('tile', 'band'), may hold values from 0 to 3
- turbine_type: int32 [1024, 1024], P('tile', 'band'), may hold values from 0 to 7
- drag_coeff: float32 [8, 16], replicated, may hold values from 0.005 to 0.05
- tke_coeff: float32 [8, 16], replicated, may hold values from 0.01 to 0.1
- cutoffs: int32 [2, 16], replicated, may hold values from 1 to 64
Outputs:
- east_out: float32 [16, 1024, 1024], P(None, 'tile', 'band')
- north_out: float32 [16, 1024, 1024], P(None, 'tile', 'band')
- theta_out: float32 [16, 1024, 1024], P(None, 'tile', 'band')
- tke_out: float32 [16, 1024, 1024], P(None, 'tile', 'band')
All inputs are finite; a program needn't handle non-finite values.
Results may differ from a plain program's by a relative error of at most 0.000082.
Values sent between devices are 32-bit elements; how exact they have to be, the bound alone decides.
A program may use at most 192 MiB of HBM per device.

v0:
```python
import functools

import jax
import jax.numpy as jnp
import ml_dtypes
import numpy as np
from jax import lax
from jax.experimental import pallas as pl
from jax.experimental.pallas import tpu as pltpu
from jax.sharding import PartitionSpec as P

KMAX = 64
MODES = 2 * KMAX
NTYPE = 8
LEV = 16
FIELDS = 3
BANDS = 8
TILES = 16
NX = 64
NY = 128
RX = 21
RY = 32
PLANES = 6
GROUPS = 4
GLEV = LEV // GROUPS
SLOTS = FIELDS * GLEV
PER = 6
PAD = 8
MESH = pl.DeviceIdType.MESH
BF = jnp.bfloat16
F32 = jnp.float32


def wavenumbers():
    index = np.arange(MODES)
    return np.where(index < KMAX, index, index - KMAX + 1)


def basis(extent, positions):
    number = wavenumbers()
    angle = 2 * np.pi * ((number[:, None] * positions[None, :]) % extent) / extent
    return np.where((np.arange(MODES) < KMAX)[:, None], np.cos(angle), np.sin(angle))


def window(length, extent, rank):
    index = np.arange(length)
    half = (KMAX + 0.5) / extent
    diagonal = ((length - 1 - 2 * index) / 2) ** 2 * np.cos(2 * np.pi * half)
    beside = index[1:] * (length - index[1:]) / 2
    _, vectors = np.linalg.eigh(np.diag(diagonal) + np.diag(beside, 1) + np.diag(beside, -1))
    vectors = vectors[:, ::-1][:, :rank]
    largest = vectors[np.argmax(np.abs(vectors) > 0.02, axis=0), np.arange(rank)]
    return vectors * np.sign(largest)


def halves(table):
    high = table.astype(np.float32).astype(ml_dtypes.bfloat16)
    low = (table - high.astype(np.float64)).astype(np.float32).astype(ml_dtypes.bfloat16)
    return high, low


def stencil_table():
    central = {1: 45.0, -1: -45.0, 2: -9.0, -2: 9.0, 3: 1.0, -3: -1.0}
    smooth = {3: 1.0, -3: 1.0, 2: -6.0, -2: -6.0, 1: 15.0, -1: 15.0, 0: -20.0}
    inner = np.zeros((NY, 2 * NY))
    outer = np.zeros((NY, 2 * NY))
    for column, taps in ((0, central), (NY, smooth)):
        for y in range(NY):
            for offset, tap in taps.items():
                at = y + offset
                if 0 <= at < NY:
                    inner[at, column + y] = tap
                elif at < 0:
                    outer[at + 3, column + y] = tap
                else:
                    outer[at - NY + 3, column + y] = tap
    return np.concatenate([inner, inner, outer, outer]).astype(ml_dtypes.bfloat16)


def make_tables():
    east_n, north_n = NX * TILES, NY * BANDS
    vx = window(NX, east_n, RX)
    vy = window(NY, north_n, RY)
    ux = [basis(east_n, NX * t + np.arange(NX)) @ vx for t in range(TILES)]
    uy = [basis(north_n, NY * b + np.arange(NY)) @ vy for b in range(BANDS)]

    block = np.zeros((PLANES * NX, 128))
    for p in range(PLANES):
        block[p * NX : (p + 1) * NX, p * RX : (p + 1) * RX] = vx
    high, low = halves(block.T)
    x_forward = np.concatenate([high, low], axis=0)
    high, low = halves(0.5 * block)
    x_back = np.concatenate([high, high, low], axis=1)

    high, low = halves(vy.T)
    y_forward = np.concatenate(
        [np.concatenate([high, high], axis=1), np.concatenate([low, 0 * low], axis=1)], axis=0
    )
    diag = np.zeros((4 * RY, 4 * NY))
    for g in range(4):
        diag[g * RY : (g + 1) * RY, g * NY : (g + 1) * NY] = vy.T
    y_back = np.concatenate(halves(diag), axis=1)

    uy_all = np.concatenate(uy, axis=1)
    m_forward = np.concatenate(halves(uy_all), axis=0)
    m_back = np.concatenate(halves(uy_all.T), axis=0)

    ux_all = np.zeros((MODES, 384))
    for t in range(TILES):
        at = 128 * (t // PER) + RX * (t % PER)
        ux_all[:, at : at + RX] = ux[t]
    k_forward = np.concatenate(halves(ux_all.T), axis=1)
    k_back = np.concatenate(halves(ux_all), axis=1)

    number = wavenumbers()
    weight_k = np.where(number == 0, 1.0, 2.0) / east_n
    weight_m = np.where(number == 0, 1.0, 2.0) / north_n
    weights = (weight_m[:, None] * weight_k[None, :]).astype(np.float32)
    number_k = np.broadcast_to(number[None, :], (8, MODES)).astype(np.int32)
    number_m = np.broadcast_to(number[:, None], (MODES, MODES)).astype(np.int32)
    return (
        x_forward,
        y_forward,
        m_forward,
        k_forward,
        k_back,
        m_back,
        y_back,
        x_back,
        stencil_table(),
        weights,
        number_k,
        number_m,
    )


def split(value):
    high = value.astype(BF)
    low = (value - high.astype(F32)).astype(BF)
    return high, low


def dot(a, b):
    return lax.dot_general(a, b, (((1,), (0,)), ((), ())), preferred_element_type=F32)


def quarters(product, rows, columns):
    return (product[:rows, :columns] + product[:rows, columns:]) + (
        product[rows:, :columns] + product[rows:, columns:]
    )


def kernel(
    wind_east,
    wind_north,
    theta_pert,
    tke_field,
    target_east,
    target_north,
    target_theta,
    turbine_count,
    turbine_type,
    drag_coeff,
    tke_coeff,
    cutoffs,
    x_forward,
    y_forward,
    m_forward,
    k_forward,
    k_back,
    m_back,
    y_back,
    x_back,
    stencil,
    weights,
    number_k,
    number_m,
    east_out,
    north_out,
    theta_out,
    tke_out,
    q0,
    q1,
    q2,
    target,
    tke,
    count,
    kind,
    partial,
    drag,
    force,
    result,
    diffs,
    y_halo,
    xs,
    xr,
    ys,
    yr,
    s1,
    r1,
    s2,
    r2,
    s3,
    r3,
    s4,
    r4,
    modes,
    in_sem,
    out_sem,
    xs_sem,
    xr_sem,
    ys_sem,
    yr_sem,
    s1_sem,
    r1_sem,
    s2_sem,
    r2_sem,
    s3_sem,
    r3_sem,
    s4_sem,
    r4_sem,
):
    band = lax.axis_index("band")
    tile = lax.axis_index("tile")

    inputs = []
    for f, source in enumerate((wind_east, wind_north, theta_pert)):
        inputs.append((source, q0.at[pl.ds(f * LEV, LEV), pl.ds(PAD, NX), :]))
    for f, source in enumerate((target_east, target_north, target_theta)):
        inputs.append((source, target.at[pl.ds(f * LEV, LEV)]))
    inputs += [(tke_field, tke), (turbine_count, count), (turbine_type, kind)]
    inputs = [
        pltpu.make_async_copy(source, into, in_sem.at[i])
        for i, (source, into) in enumerate(inputs)
    ]
    for copy in inputs:
        copy.start()

    @pl.when(tile == 0)
    def _():
        xr[:, 0] = jnp.zeros((3, GROUPS, SLOTS, 4, 128), F32)

    @pl.when(tile == TILES - 1)
    def _():
        xr[:, 1] = jnp.zeros((3, GROUPS, SLOTS, 4, 128), F32)

    @pl.when(band == 0)
    def _():
        yr[:, 0] = jnp.zeros((3, GROUPS, NX, 128), F32)

    @pl.when(band == BANDS - 1)
    def _():
        yr[:, 1] = jnp.zeros((3, GROUPS, NX, 128), F32)

    barrier = pltpu.get_barrier_semaphore()
    for step in range(1, BANDS):
        pl.semaphore_signal(
            barrier, inc=1, device_id={"band": lax.rem(band + step, BANDS)}, device_id_type=MESH
        )
    for step in range(1, TILES):
        pl.semaphore_signal(
            barrier, inc=1, device_id={"tile": lax.rem(tile + step, TILES)}, device_id_type=MESH
        )

    lane = lax.broadcasted_iota(jnp.int32, (NX, 128), 1)
    low_lane = lax.rem(lane, 6) < 3


    def pack_edges(turn, group, slot, plane):
        xs[turn, 0, group, slot, 0:3, :] = plane[0:3]
        xs[turn, 1, group, slot, 0:3, :] = plane[NX - 3 : NX]
        first = slot * 6
        mine = jnp.logical_and(lane >= first, lane < first + 6)
        moved = pltpu.roll(plane, first + 3, 1)
        before = jnp.where(slot == 0, jnp.zeros((NX, 128), F32), ys[turn, group])
        ys[turn, group] = jnp.where(mine, moved, before)

    def x_copy(turn, group, side):
        return pltpu.make_async_remote_copy(
            src_ref=xs.at[turn, side, group],
            dst_ref=xr.at[turn, 1 - side, group],
            send_sem=xs_sem.at[turn, side, group],
            recv_sem=xr_sem.at[turn, 1 - side, group],
            device_id={"tile": tile + (1 if side else -1)},
            device_id_type=MESH,
        )

    def y_copy(turn, group, side):
        return pltpu.make_async_remote_copy(
            src_ref=ys.at[turn, group],
            dst_ref=yr.at[turn, 1 - side, group],
            send_sem=ys_sem.at[turn, side, group],
            recv_sem=yr_sem.at[turn, 1 - side, group],
            device_id={"band": band + (1 if side else -1)},
            device_id_type=MESH,
        )

    has = (
        (tile > 0, band > 0),
        (tile < TILES - 1, band < BANDS - 1),
    )

    def send_edges(turn, group):
        for side in range(2):

            @pl.when(has[side][0])
            def _():
                x_copy(turn, group, side).start()

            @pl.when(has[side][1])
            def _():
                y_copy(turn, group, side).start()

    def await_edges(turn, group):
        for side in range(2):

            @pl.when(has[side][0])
            def _():
                x_copy(turn, group, 1 - side).wait_recv()

            @pl.when(has[side][1])
            def _():
                y_copy(turn, group, 1 - side).wait_recv()

        y_halo[...] = jnp.where(low_lane, yr[turn, 0, group], yr[turn, 1, group])

    def edges_sent(turn, group):
        for side in range(2):

            @pl.when(has[side][0])
            def _():
                x_copy(turn, group, side).wait_send()

            @pl.when(has[side][1])
            def _():
                y_copy(turn, group, side).wait_send()


    def advance(turn, group, source, finish):
        @pl.loop(0, GLEV)
        def _(inner):
            level = group * GLEV + inner
            rows = []
            for f in range(FIELDS):
                slot = f * GLEV + inner
                plane = f * LEV + level
                source[plane, PAD - 3 : PAD, :] = xr[turn, 0, group, slot, 0:3, :]
                source[plane, PAD + NX : PAD + NX + 3, :] = xr[turn, 1, group, slot, 0:3, :]
                high, low = split(source[plane, PAD : PAD + NX, :])
                halo_high, halo_low = split(pltpu.roll(y_halo[...], 128 - slot * 6, 1))
                rows.append(jnp.concatenate([high, low, halo_high, halo_low], axis=1))
            diffs[...] = dot(jnp.concatenate(rows, axis=0), stencil[...])
            chunk = 16
            for at in range(0, NX, chunk):
                east = source[level, PAD + at : PAD + at + chunk, :] * (1.0 / 60.0)
                north = source[LEV + level, PAD + at : PAD + at + chunk, :] * (1.0 / 60.0)
                east_size = jnp.abs(east)
                north_size = jnp.abs(north)
                for f in range(FIELDS):
                    plane = f * LEV + level

                    def cell(offset):
                        return source[plane, PAD + at + offset : PAD + at + offset + chunk, :]

                    up1, up2, up3 = cell(1), cell(2), cell(3)
                    down1, down2, down3 = cell(-1), cell(-2), cell(-3)
                    central = 45.0 * (up1 - down1) - 9.0 * (up2 - down2) + (up3 - down3)
                    smooth = (
                        (up3 + down3)
                        - 6.0 * (up2 + down2)
                        + 15.0 * (up1 + down1)
                        - 20.0 * cell(0)
                    )
                    central_y = diffs[f * NX + at : f * NX + at + chunk, 0:NY]
                    smooth_y = diffs[f * NX + at : f * NX + at + chunk, NY : 2 * NY]
                    value = (east_size * smooth - east * central) + (
                        north_size * smooth_y - north * central_y
                    )
                    finish(f, level, plane, at, chunk, value)


    def turbines(group):
        counts = count[...].astype(F32)
        kinds = kind[...]

        @pl.loop(0, GLEV)
        def _(inner):
            level = group * GLEV + inner
            rate = jnp.full((NX, NY), drag_coeff[0, level])
            growth = jnp.full((NX, NY), tke_coeff[0, level])
            for k in range(1, NTYPE):
                here = kinds == k
                rate = jnp.where(here, drag_coeff[k, level], rate)
                growth = jnp.where(here, tke_coeff[k, level], growth)
            east = q0[level, PAD : PAD + NX, :]
            north = q0[LEV + level, PAD : PAD + NX, :]
            speed = jnp.sqrt(east * east + north * north)
            rate = counts * rate * speed
            tke[level] = tke[level] + counts * growth * speed * speed * speed
            drag[level] = -(rate * east)
            drag[LEV + level] = -(rate * north)

    def tke_copy(group):
        rows = pl.ds(group * GLEV, GLEV)
        return pltpu.make_async_copy(tke.at[rows], tke_out.at[rows], out_sem.at[3, group])


    for copy in inputs[:3]:
        copy.wait()

    @pl.loop(0, GROUPS)
    def _(group):
        @pl.loop(0, GLEV)
        def _(inner):
            for f in range(FIELDS):
                plane = f * LEV + group * GLEV + inner
                pack_edges(0, group, f * GLEV + inner, q0[plane, PAD : PAD + NX, :])

    for copy in inputs[3:6]:
        copy.wait()

    @pl.loop(0, BANDS)
    def _(to):
        rows = []
        for f in range(FIELDS):
            part = pl.ds(f * LEV + 2 * to, 2)
            gap = target[part] - q0[part, PAD : PAD + NX, :]
            rows.append(gap.reshape(2 * NX, NY))
        high, low = split(jnp.concatenate(rows, axis=0))
        along_x = quarters(dot(x_forward[...], jnp.concatenate([high, low], axis=1)), 128, NY)
        both = lax.dot_general(
            y_forward[...],
            jnp.concatenate(split(along_x), axis=1),
            (((1,), (1,)), ((), ())),
            preferred_element_type=F32,
        )
        s1[to] = both[:RY] + both[RY:]

    pl.semaphore_wait(barrier, BANDS - 1 + TILES - 1)

    @pl.loop(0, GROUPS)
    def _(group):
        send_edges(0, group)

    def exchange(axis, count, me, source, into, send_sem, recv_sem, step):
        other = lax.rem(me + step, count)
        return (
            other,
            pltpu.make_async_remote_copy(
                src_ref=source.at[other],
                dst_ref=into.at[me],
                send_sem=send_sem.at[other],
                recv_sem=recv_sem.at[me],
                device_id={axis: other},
                device_id_type=MESH,
            ),
        )

    def send_all(axis, count, me, source, into, send_sem, recv_sem):
        for step in range(1, count):
            exchange(axis, count, me, source, into, send_sem, recv_sem, step)[1].start()
        into[me] = source[me]

    def receive_all(axis, count, me, source, into, send_sem, recv_sem):
        for step in range(1, count):
            other = lax.rem(me + step, count)
            pltpu.make_async_remote_copy(
                src_ref=source.at[other],
                dst_ref=into.at[other],
                send_sem=send_sem.at[other],
                recv_sem=recv_sem.at[other],
                device_id={axis: other},
                device_id_type=MESH,
            ).wait_recv()

    def sent_all(axis, count, me, source, into, send_sem, recv_sem):
        for step in range(1, count):
            exchange(axis, count, me, source, into, send_sem, recv_sem, step)[1].wait_send()

    phase1 = ("band", BANDS, band, s1, r1, s1_sem, r1_sem)
    phase2 = ("tile", TILES, tile, s2, r2, s2_sem, r2_sem)
    phase3 = ("tile", TILES, tile, s3, r3, s3_sem, r3_sem)
    phase4 = ("band", BANDS, band, s4, r4, s4_sem, r4_sem)

    send_all(*phase1)
    for copy in inputs[6:]:
        copy.wait()

    def first_finish(f, level, plane, at, chunk, value):
        if f < 2:
            value = value + drag[plane, at : at + chunk, :]
        partial[plane, at : at + chunk, :] = value

    def first_stage(group):
        turbines(group)
        tke_copy(group).start()
        await_edges(0, group)
        advance(0, group, q0, first_finish)

    first_stage(0)
    receive_all(*phase1)

    received = r1[...].reshape(BANDS * RY, 128)
    columns = jnp.concatenate(split(received), axis=1)
    s2[...] = quarters(dot(m_forward[...], columns), MODES, 128).reshape(TILES, 8, 128)
    send_all(*phase2)
    first_stage(1)
    receive_all(*phase2)

    lane8 = lax.broadcasted_iota(jnp.int32, (8, 128), 1)
    inside = [
        jnp.logical_and(lane8 >= RX * i, lane8 < RX * (i + 1)) for i in range(PER)
    ]
    blocks = [r2[t] for t in range(TILES)]
    rows = []
    for p in range(PLANES):
        parts = []
        for first in range(0, TILES, PER):
            value = jnp.zeros((8, 128), F32)
            for i, t in enumerate(range(first, min(first + PER, TILES))):
                moved = pltpu.roll(blocks[t], (RX * (i - p)) % 128, 1)
                value = jnp.where(inside[i], moved, value)
            parts.append(value)
        rows.append(jnp.concatenate(parts, axis=1))
    packed = jnp.concatenate(split(jnp.concatenate(rows, axis=0)), axis=0)
    spectra = quarters(dot(packed, k_forward[...]), 8 * PLANES, MODES)
    mine = pl.ds(pl.multiple_of(tile * 8, 8), 8)
    weight = weights[mine, :]
    east_number = number_k[...]
    north_number = number_m[mine, :]
    masks = []
    for inner in range(2):
        keep = jnp.logical_and(
            east_number <= cutoffs[0, 2 * band + inner],
            north_number <= cutoffs[1, 2 * band + inner],
        )
        masks.append(jnp.where(keep, weight, 0.0))
    spectra = spectra * jnp.concatenate(masks * FIELDS, axis=0)
    high, low = split(spectra)
    back = dot(jnp.concatenate([high, low], axis=0), k_back[...])
    back = quarters(back, 8 * PLANES, 384)
    for t in range(TILES):
        first = 128 * (t // PER)
        value = jnp.zeros((8, 128), F32)
        for p in range(PLANES):
            moved = pltpu.roll(
                back[8 * p : 8 * p + 8, first : first + 128], (RX * (p - t % PER)) % 128, 1
            )
            value = jnp.where(inside[p], moved, value)
        s3[t] = value
    send_all(*phase3)
    first_stage(2)
    receive_all(*phase3)

    received = r3[...].reshape(MODES, 128)
    back = quarters(dot(m_back[...], jnp.concatenate(split(received), axis=1)), BANDS * RY, 128)
    s4[...] = back.reshape(BANDS, RY, 128)
    send_all(*phase4)
    first_stage(3)
    receive_all(*phase4)

    for half in range(2):
        columns = r4[4 * half : 4 * half + 4].reshape(4 * RY, 128).T
        wide = dot(jnp.concatenate(split(columns), axis=0), y_back[...])
        wide = quarters(wide, 128, 4 * NY)
        for i in range(4):
            modes[4 * half + i] = wide[:, i * NY : (i + 1) * NY]

    @pl.loop(0, GROUPS)
    def _(group):
        for pair in range(2):
            high, low = split(modes[2 * group + pair])
            smooth_part = dot(x_back[...], jnp.concatenate([high, low, high], axis=0))
            for f in range(FIELDS):
                for inner in range(2):
                    plane = f * LEV + group * GLEV + 2 * pair + inner
                    at = (2 * f + inner) * NX
                    nudge = smooth_part[at : at + NX]
                    if f < 2:
                        force[plane] = nudge + drag[plane]
                    else:
                        force[plane] = nudge
                    value = q0[plane, PAD : PAD + NX, :] + (1.0 / 3.0) * (nudge + partial[plane])
                    q1[plane, PAD : PAD + NX, :] = value
                    pack_edges(1, group, f * GLEV + 2 * pair + inner, value)
        send_edges(1, group)

    def second_finish(f, level, plane, at, chunk, value):
        q2[plane, PAD + at : PAD + at + chunk, :] = q0[
            plane, PAD + at : PAD + at + chunk, :
        ] + 0.5 * (value + force[plane, at : at + chunk, :])

    @pl.loop(0, GROUPS)
    def _(group):
        await_edges(1, group)
        advance(1, group, q1, second_finish)

        @pl.loop(0, GLEV)
        def _(inner):
            for f in range(FIELDS):
                plane = f * LEV + group * GLEV + inner
                pack_edges(2, group, f * GLEV + inner, q2[plane, PAD : PAD + NX, :])

        send_edges(2, group)

    def third_finish(f, level, plane, at, chunk, value):
        result[plane, at : at + chunk, :] = q0[plane, PAD + at : PAD + at + chunk, :] + (
            value + force[plane, at : at + chunk, :]
        )

    def out_copy(f, group):
        rows = pl.ds(group * GLEV, GLEV)
        into = (east_out, north_out, theta_out)[f]
        return pltpu.make_async_copy(
            result.at[pl.ds(f * LEV + group * GLEV, GLEV)], into.at[rows], out_sem.at[f, group]
        )

    @pl.loop(0, GROUPS)
    def _(group):
        await_edges(2, group)
        advance(2, group, q2, third_finish)
        for f in range(FIELDS):
            out_copy(f, group).start()

    for phase in (phase1, phase2, phase3, phase4):
        sent_all(*phase)

    @pl.loop(0, GROUPS)
    def _(group):
        for turn in range(3):
            edges_sent(turn, group)
        for f in range(FIELDS):
            out_copy(f, group).wait()
        tke_copy(group).wait()


def shards(*arguments):
    tables = [jnp.asarray(table) for table in make_tables()]
    field = jax.ShapeDtypeStruct((LEV, NX, NY), F32)
    anywhere = pl.BlockSpec(memory_space=pl.ANY)
    smem = pl.BlockSpec(memory_space=pltpu.SMEM)
    vmem = pl.BlockSpec(memory_space=pltpu.VMEM)
    padded = pltpu.VMEM((FIELDS * LEV, NX + 2 * PAD, NY), F32)
    planes = pltpu.VMEM((FIELDS * LEV, NX, NY), F32)
    dma = pltpu.SemaphoreType.DMA
    return pl.pallas_call(
        kernel,
        out_shape=(field,) * 4,
        in_specs=[anywhere] * 9 + [smem] * 3 + [vmem] * len(tables),
        out_specs=(anywhere,) * 4,
        scratch_shapes=[
            padded,
            padded,
            padded,
            planes,
            pltpu.VMEM((LEV, NX, NY), F32),
            pltpu.VMEM((NX, NY), jnp.int32),
            pltpu.VMEM((NX, NY), jnp.int32),
            planes,
            pltpu.VMEM((2 * LEV, NX, NY), F32),
            planes,
            planes,
            pltpu.VMEM((FIELDS * NX, 2 * NY), F32),
            pltpu.VMEM((NX, 128), F32),
            pltpu.VMEM((3, 2, GROUPS, SLOTS, 4, 128), F32),
            pltpu.VMEM((3, 2, GROUPS, SLOTS, 4, 128), F32),
            pltpu.VMEM((3, GROUPS, NX, 128), F32),
            pltpu.VMEM((3, 2, GROUPS, NX, 128), F32),
            pltpu.VMEM((BANDS, RY, 128), F32),
            pltpu.VMEM((BANDS, RY, 128), F32),
            pltpu.VMEM((TILES, 8, 128), F32),
            pltpu.VMEM((TILES, 8, 128), F32),
            pltpu.VMEM((TILES, 8, 128), F32),
            pltpu.VMEM((TILES, 8, 128), F32),
            pltpu.VMEM((BANDS, RY, 128), F32),
            pltpu.VMEM((BANDS, RY, 128), F32),
            pltpu.VMEM((BANDS, 128, NY), F32),
            dma((9,)),
            dma((4, GROUPS)),
            dma((3, 2, GROUPS)),
            dma((3, 2, GROUPS)),
            dma((3, 2, GROUPS)),
            dma((3, 2, GROUPS)),
            dma((BANDS,)),
            dma((BANDS,)),
            dma((TILES,)),
            dma((TILES,)),
            dma((TILES,)),
            dma((TILES,)),
            dma((BANDS,)),
            dma((BANDS,)),
        ],
        compiler_params=pltpu.CompilerParams(
            collective_id=0, has_side_effects=True, vmem_limit_bytes=40 * 1024 * 1024
        ),
        cost_estimate=pl.CostEstimate(
            flops=10**9, bytes_accessed=6 * 2**20, transcendentals=LEV * NX * NY
        ),
        name="step",
    )(*arguments, *tables)


def solution(mesh):
    field = P(None, "tile", "band")
    column = P("tile", "band")
    in_specs = (field,) * 7 + (column,) * 2 + (P(),) * 3
    return jax.shard_map(
        shards, mesh=mesh, in_specs=in_specs, out_specs=(field,) * 4, check_vma=False
    )
```

profile of v0, /device:TPU:2, one launch (start us, length us, event | category | flops | bytes accessed | tf_op | source)
XLA Modules:
  0.0 73.7 jit_solution(14450265193152369428)
XLA Ops:
  0.6 0.0 copy-start.22
  0.6 0.7 copy-done.22
  1.3 0.0 copy-start
  1.3 1.0 %copy-done = f32[16,64,128]{2,1,0:T(8,128)S(1)} copy-done((f32[16,64,128]{2,1,0:T(8,128)S(1)}, f32[16,64,128]{2,1,0:T(8,128)}, u32[]{:S(2)}) %copy-start) | copy-done | bytes 524312
  2.4 0.0 copy-start.1
  2.4 1.0 %copy-done.1 = f32[16,64,128]{2,1,0:T(8,128)S(1)} copy-done((f32[16,64,128]{2,1,0:T(8,128)S(1)}, f32[16,64,128]{2,1,0:T(8,128)}, u32[]{:S(2)}) %copy-start.1) | copy-done | bytes 524312
  3.4 1.0 %copy-done.2 = f32[16,64,128]{2,1,0:T(8,128)S(1)} copy-done((f32[16,64,128]{2,1,0:T(8,128)S(1)}, f32[16,64,128]{2,1,0:T(8,128)}, u32[]{:S(2)}) %copy-start.2) | copy-done | bytes 524312
  4.5 1.0 %copy-done.3 = f32[16,64,128]{2,1,0:T(8,128)S(1)} copy-done((f32[16,64,128]{2,1,0:T(8,128)S(1)}, f32[16,64,128]{2,1,0:T(8,128)}, u32[]{:S(2)}) %copy-start.3) | copy-done | bytes 524312
  5.5 1.0 %copy-done.4 = f32[16,64,128]{2,1,0:T(8,128)S(1)} copy-done((f32[16,64,128]{2,1,0:T(8,128)S(1)}, f32[16,64,128]{2,1,0:T(8,128)}, u32[]{:S(2)}) %copy-start.4) | copy-done | bytes 524312
  6.5 1.0 %copy-done.5 = f32[16,64,128]{2,1,0:T(8,128)S(1)} copy-done((f32[16,64,128]{2,1,0:T(8,128)S(1)}, f32[16,64,128]{2,1,0:T(8,128)}, u32[]{:S(2)}) %copy-start.5) | copy-done | bytes 524312
  7.6 1.0 %copy-done.6 = f32[16,64,128]{2,1,0:T(8,128)S(1)} copy-done((f32[16,64,128]{2,1,0:T(8,128)S(1)}, f32[16,64,128]{2,1,0:T(8,128)}, u32[]{:S(2)}) %copy-start.6) | copy-done | bytes 524312
  8.6 1.0 %copy-done.7 = bf16[384,384]{1,0:T(8,128)(2,1)S(1)} copy-done((bf16[384,384]{1,0:T(8,128)(2,1)S(1)}, bf16[384,384]{1,0:T(8,128)(2,1)}, u32[]{:S(2)}) %copy-start.7) | copy-done | bytes 294936
  9.6 0.9 %copy-done.8 = bf16[512,256]{1,0:T(8,128)(2,1)S(1)} copy-done((bf16[512,256]{1,0:T(8,128)(2,1)S(1)}, bf16[512,256]{1,0:T(8,128)(2,1)}, u32[]{:S(2)}) %copy-start.8) | copy-done | bytes 262168
  10.5 0.9 %copy-done.9 = bf16[128,1024]{1,0:T(8,128)(2,1)S(1)} copy-done((bf16[128,1024]{1,0:T(8,128)(2,1)S(1)}, bf16[128,1024]{1,0:T(8,128)(2,1)}, u32[]{:S(2)}) %copy-start.9) | copy-done | bytes 262168
  11.5 0.9 %copy-done.10 = bf16[128,768]{1,0:T(8,128)(2,1)S(1)} copy-done((bf16[128,768]{1,0:T(8,128)(2,1)S(1)}, bf16[128,768]{1,0:T(8,128)(2,1)}, u32[]{:S(2)}) %copy-start.10) | copy-done | bytes 196632
  12.4 0.9 %copy-done.11 = bf16[384,256]{1,0:T(8,128)(2,1)S(1)} copy-done((bf16[384,256]{1,0:T(8,128)(2,1)S(1)}, bf16[384,256]{1,0:T(8,128)(2,1)}, u32[]{:S(2)}) %copy-start.11) | copy-done | bytes 196632
  13.3 0.9 %copy-done.12 = bf16[256,384]{1,0:T(8,128)(2,1)S(1)} copy-done((bf16[256,384]{1,0:T(8,128)(2,1)S(1)}, bf16[256,384]{1,0:T(8,128)(2,1)}, u32[]{:S(2)}) %copy-start.12) | copy-done | bytes 196632
  14.3 0.9 %copy-done.13 = bf16[512,128]{1,0:T(8,128)(2,1)S(1)} copy-done((bf16[512,128]{1,0:T(8,128)(2,1)S(1)}, bf16[512,128]{1,0:T(8,128)(2,1)}, u32[]{:S(2)}) %copy-start.13) | copy-done | bytes 131096
  15.2 0.9 %copy-done.14 = bf16[256,256]{1,0:T(8,128)(2,1)S(1)} copy-done((bf16[256,256]{1,0:T(8,128)(2,1)S(1)}, bf16[256,256]{1,0:T(8,128)(2,1)}, u32[]{:S(2)}) %copy-start.14) | copy-done | bytes 131096
  16.1 0.8 %copy-done.15 = s32[128,128]{1,0:T(8,128)S(1)} copy-done((s32[128,128]{1,0:T(8,128)S(1)}, s32[128,128]{1,0:T(8,128)}, u32[]{:S(2)}) %copy-start.15) | copy-done | bytes 65560
  16.9 0.8 %copy-done.16 = f32[128,128]{1,0:T(8,128)S(1)} copy-done((f32[128,128]{1,0:T(8,128)S(1)}, f32[128,128]{1,0:T(8,128)}, u32[]{:S(2)}) %copy-start.16) | copy-done | bytes 65560
  17.8 0.8 %copy-done.17 = s32[64,128]{1,0:T(8,128)S(1)} copy-done((s32[64,128]{1,0:T(8,128)S(1)}, s32[64,128]{1,0:T(8,128)}, u32[]{:S(2)}) %copy-start.17) | copy-done | bytes 32792
  18.5 0.8 %copy-done.18 = s32[64,128]{1,0:T(8,128)S(1)} copy-done((s32[64,128]{1,0:T(8,128)S(1)}, s32[64,128]{1,0:T(8,128)}, u32[]{:S(2)}) %copy-start.18) | copy-done | bytes 32792
  19.3 0.8 %copy-done.19 = bf16[64,256]{1,0:T(8,128)(2,1)S(1)} copy-done((bf16[64,256]{1,0:T(8,128)(2,1)S(1)}, bf16[64,256]{1,0:T(8,128)(2,1)}, u32[]{:S(2)}) %copy-start.19) | copy-done | bytes 32792
  20.0 0.7 copy-done.20
  20.7 0.7 copy-done.21
  21.4 0.7 copy-done.23
  22.1 48.4 %step.1 = (f32[16,64,128]{2,1,0:T(8,128)S(1)}, f32[16,64,128]{2,1,0:T(8,128)S(1)}, f32[16,64,128]{2,1,0:T(8,128)S(1)}, f32[16,64,128]{2,1,0:T(8,128)S(1)}) custom-call(f32[16,64,128]{2,1,0:T(8,128)S(1)} %copy-done, f32[16,64,128]{2,1,0:T(8,128)S(1)} %copy-done.1, f32[16,64,128]{2,1,0:T(8,128)S(1)} %copy-done.2, f32[16,64,128]{2,1,0:T(8,128)S(1)} %copy-done.3, ...), custom_call_target="tpu_custom_call" | custom-call | flops 1000000000 | bytes 6291456 | tf_op jit(solution)/shard_map/step/pallas_call | solution.py:646
  70.5 0.8 %copy.32 = f32[16,64,128]{2,1,0:T(8,128)} copy(f32[16,64,128]{2,1,0:T(8,128)S(1)} %get-tuple-element.8) | data formatting | bytes 1048576
  71.3 0.8 %copy.33 = f32[16,64,128]{2,1,0:T(8,128)} copy(f32[16,64,128]{2,1,0:T(8,128)S(1)} %get-tuple-element.9) | data formatting | bytes 1048576
  72.1 0.8 %copy.34 = f32[16,64,128]{2,1,0:T(8,128)} copy(f32[16,64,128]{2,1,0:T(8,128)S(1)} %get-tuple-element.10) | data formatting | bytes 1048576
  72.9 0.8 %copy.35 = f32[16,64,128]{2,1,0:T(8,128)} copy(f32[16,64,128]{2,1,0:T(8,128)S(1)} %get-tuple-element.11) | data formatting | bytes 1048576
  (21 shorter events, 0.0 us)
Async XLA Ops:
  0.6 0.7 copy-start.22
  1.3 1.0 %copy-start = (f32[16,64,128]{2,1,0:T(8,128)S(1)}, f32[16,64,128]{2,1,0:T(8,128)}, u32[]{:S(2)}) copy-start(f32[16,64,128]{2,1,0:T(8,128)} %wind_east.1) | copy-start | bytes 1572868
  2.4 1.0 %copy-start.1 = (f32[16,64,128]{2,1,0:T(8,128)S(1)}, f32[16,64,128]{2,1,0:T(8,128)}, u32[]{:S(2)}) copy-start(f32[16,64,128]{2,1,0:T(8,128)} %wind_north.1) | copy-start | bytes 1572868
  3.4 1.0 %copy-start.2 = (f32[16,64,128]{2,1,0:T(8,128)S(1)}, f32[16,64,128]{2,1,0:T(8,128)}, u32[]{:S(2)}) copy-start(f32[16,64,128]{2,1,0:T(8,128)} %theta_pert.1) | copy-start | bytes 1572868
  4.5 1.0 %copy-start.3 = (f32[16,64,128]{2,1,0:T(8,128)S(1)}, f32[16,64,128]{2,1,0:T(8,128)}, u32[]{:S(2)}) copy-start(f32[16,64,128]{2,1,0:T(8,128)} %tke_field.1) | copy-start | bytes 1572868
  5.5 1.0 %copy-start.4 = (f32[16,64,128]{2,1,0:T(8,128)S(1)}, f32[16,64,128]{2,1,0:T(8,128)}, u32[]{:S(2)}) copy-start(f32[16,64,128]{2,1,0:T(8,128)} %target_east.1) | copy-start | bytes 1572868
  6.5 1.0 %copy-start.5 = (f32[16,64,128]{2,1,0:T(8,128)S(1)}, f32[16,64,128]{2,1,0:T(8,128)}, u32[]{:S(2)}) copy-start(f32[16,64,128]{2,1,0:T(8,128)} %target_north.1) | copy-start | bytes 1572868
  7.6 1.0 %copy-start.6 = (f32[16,64,128]{2,1,0:T(8,128)S(1)}, f32[16,64,128]{2,1,0:T(8,128)}, u32[]{:S(2)}) copy-start(f32[16,64,128]{2,1,0:T(8,128)} %target_theta.1) | copy-start | bytes 1572868
  8.6 1.0 %copy-start.7 = (bf16[384,384]{1,0:T(8,128)(2,1)S(1)}, bf16[384,384]{1,0:T(8,128)(2,1)}, u32[]{:S(2)}) copy-start(bf16[384,384]{1,0:T(8,128)(2,1)} %constant.31.clone.x_back) | copy-start | bytes 884740
  9.6 0.9 %copy-start.8 = (bf16[512,256]{1,0:T(8,128)(2,1)S(1)}, bf16[512,256]{1,0:T(8,128)(2,1)}, u32[]{:S(2)}) copy-start(bf16[512,256]{1,0:T(8,128)(2,1)} %constant.32.clone.stencil) | copy-start | bytes 786436
  10.5 0.9 %copy-start.9 = (bf16[128,1024]{1,0:T(8,128)(2,1)S(1)}, bf16[128,1024]{1,0:T(8,128)(2,1)}, u32[]{:S(2)}) copy-start(bf16[128,1024]{1,0:T(8,128)(2,1)} %constant.30.clone.y_back) | copy-start | bytes 786436
  11.5 0.9 %copy-start.10 = (bf16[128,768]{1,0:T(8,128)(2,1)S(1)}, bf16[128,768]{1,0:T(8,128)(2,1)}, u32[]{:S(2)}) copy-start(bf16[128,768]{1,0:T(8,128)(2,1)} %constant.28.clone.k_back) | copy-start | bytes 589828
  12.4 0.9 %copy-start.11 = (bf16[384,256]{1,0:T(8,128)(2,1)S(1)}, bf16[384,256]{1,0:T(8,128)(2,1)}, u32[]{:S(2)}) copy-start(bf16[384,256]{1,0:T(8,128)(2,1)} %constant.27.clone.k_forward) | copy-start | bytes 589828
  13.3 0.9 %copy-start.12 = (bf16[256,384]{1,0:T(8,128)(2,1)S(1)}, bf16[256,384]{1,0:T(8,128)(2,1)}, u32[]{:S(2)}) copy-start(bf16[256,384]{1,0:T(8,128)(2,1)} %constant.24.clone.x_forward) | copy-start | bytes 589828
  14.3 0.9 %copy-start.13 = (bf16[512,128]{1,0:T(8,128)(2,1)S(1)}, bf16[512,128]{1,0:T(8,128)(2,1)}, u32[]{:S(2)}) copy-start(bf16[512,128]{1,0:T(8,128)(2,1)} %constant.29.clone.m_back) | copy-start | bytes 393220
  15.2 0.9 %copy-start.14 = (bf16[256,256]{1,0:T(8,128)(2,1)S(1)}, bf16[256,256]{1,0:T(8,128)(2,1)}, u32[]{:S(2)}) copy-start(bf16[256,256]{1,0:T(8,128)(2,1)} %constant.26.clone.m_forward) | copy-start | bytes 393220
  16.1 0.8 %copy-start.15 = (s32[128,128]{1,0:T(8,128)S(1)}, s32[128,128]{1,0:T(8,128)}, u32[]{:S(2)}) copy-start(s32[128,128]{1,0:T(8,128)} %constant.35.clone.number_m) | copy-start | bytes 196612
  16.9 0.8 %copy-start.16 = (f32[128,128]{1,0:T(8,128)S(1)}, f32[128,128]{1,0:T(8,128)}, u32[]{:S(2)}) copy-start(f32[128,128]{1,0:T(8,128)} %constant.33.clone.weights) | copy-start | bytes 196612
  17.8 0.8 %copy-start.17 = (s32[64,128]{1,0:T(8,128)S(1)}, s32[64,128]{1,0:T(8,128)}, u32[]{:S(2)}) copy-start(s32[64,128]{1,0:T(8,128)} %turbine_count.1) | copy-start | bytes 98308
  18.5 0.8 %copy-start.18 = (s32[64,128]{1,0:T(8,128)S(1)}, s32[64,128]{1,0:T(8,128)}, u32[]{:S(2)}) copy-start(s32[64,128]{1,0:T(8,128)} %turbine_type.1) | copy-start | bytes 98308
  19.3 0.8 %copy-start.19 = (bf16[64,256]{1,0:T(8,128)(2,1)S(1)}, bf16[64,256]{1,0:T(8,128)(2,1)}, u32[]{:S(2)}) copy-start(bf16[64,256]{1,0:T(8,128)(2,1)} %constant.25.clone.y_forward) | copy-start | bytes 98308
  20.0 0.7 copy-start.20
  20.7 0.7 copy-start.21
  21.4 0.7 copy-start.23
where the time goes:
time: 74.7 us; the launch traced here: 73.7 us
  Pallas kernels  48.4 us (65%)
  local copies, waits for them, and re-layouts  24.6 us (33%)
    pallas_call x1, Pallas kernels, shards(): pl.pallas_call(kernel, out_shape=(field,) * 4, in_specs=[anywhere] * 9 +...  48.4 us
    unnamed x52, local copies, waits for them, and re-layouts  24.6 us

commit v1 on v0

--- a/solution.py
+++ b/solution.py
@@ -26,6 +26,7 @@
 SLOTS = FIELDS * GLEV
 PER = 6
 PAD = 8
+TABLES = 14
 MESH = pl.DeviceIdType.MESH
 BF = jnp.bfloat16
 F32 = jnp.float32
@@ -81,6 +82,10 @@
     east_n, north_n = NX * TILES, NY * BANDS
     vx = window(NX, east_n, RX)
     vy = window(NY, north_n, RY)
+    wx = window(NX + 6, east_n, RX)
+    wy = window(NY + 6, north_n, RY)
+    cells_x = np.arange(NX + 6) - 3
+    cells_y = np.arange(NY + 6) - 3
     ux = [basis(east_n, NX * t + np.arange(NX)) @ vx for t in range(TILES)]
     uy = [basis(north_n, NY * b + np.arange(NY)) @ vy for b in range(BANDS)]
 
@@ -89,27 +94,49 @@
         block[p * NX : (p + 1) * NX, p * RX : (p + 1) * RX] = vx
     high, low = halves(block.T)
     x_forward = np.concatenate([high, low], axis=0)
-    high, low = halves(0.5 * block)
+    rows = PLANES * NX
+    block = np.zeros((rows + PLANES * 8, 128))
+    for p in range(PLANES):
+        columns = slice(p * RX, (p + 1) * RX)
+        block[p * NX : (p + 1) * NX, columns] = 0.5 * wx[3 : NX + 3]
+        block[rows + 8 * p : rows + 8 * p + 3, columns] = 0.5 * wx[:3]
+        block[rows + 8 * p + 4 : rows + 8 * p + 7, columns] = 0.5 * wx[NX + 3 :]
+    high, low = halves(block)
     x_back = np.concatenate([high, high, low], axis=1)
+    shared = sum(block[p * NX : (p + 1) * NX] for p in range(PLANES))
+    high, low = halves(shared)
+    x_shared = np.concatenate([high, high, low], axis=1)
 
     high, low = halves(vy.T)
     y_forward = np.concatenate(
         [np.concatenate([high, high], axis=1), np.concatenate([low, 0 * low], axis=1)], axis=0
     )
-    diag = np.zeros((4 * RY, 4 * NY))
+    inner_y, outer_y = wy[3 : NY + 3].T, np.zeros((RY, NY))
+    outer_y[:, : 6 * SLOTS] = np.tile(np.concatenate([wy[:3], wy[NY + 3 :]]).T, (1, SLOTS))
+    diag = np.zeros((4 * RY, 8 * NY))
     for g in range(4):
-        diag[g * RY : (g + 1) * RY, g * NY : (g + 1) * NY] = vy.T
+        diag[g * RY : (g + 1) * RY, g * NY : (g + 1) * NY] = inner_y
+        diag[g * RY : (g + 1) * RY, (4 + g) * NY : (5 + g) * NY] = outer_y
     y_back = np.concatenate(halves(diag), axis=1)
+    own_slot = np.zeros((2, 128, 128), np.float32)
+    for pair in range(2):
+        for p in range(PLANES):
+            slot = (p // 2) * GLEV + 2 * pair + p % 2
+            own_slot[pair, p * RX : (p + 1) * RX, 6 * slot : 6 * slot + 6] = 1
 
     uy_all = np.concatenate(uy, axis=1)
     m_forward = np.concatenate(halves(uy_all), axis=0)
-    m_back = np.concatenate(halves(uy_all.T), axis=0)
+    uy = [basis(north_n, NY * b + cells_y) @ wy for b in range(BANDS)]
+    m_back = np.concatenate(halves(np.concatenate(uy, axis=1).T), axis=0)
 
     ux_all = np.zeros((MODES, 384))
     for t in range(TILES):
         at = 128 * (t // PER) + RX * (t % PER)
         ux_all[:, at : at + RX] = ux[t]
     k_forward = np.concatenate(halves(ux_all.T), axis=1)
+    for t in range(TILES):
+        at = 128 * (t // PER) + RX * (t % PER)
+        ux_all[:, at : at + RX] = basis(east_n, NX * t + cells_x) @ wx
     k_back = np.concatenate(halves(ux_all), axis=1)
 
     number = wavenumbers()
@@ -127,6 +154,8 @@
         m_back,
         y_back,
         x_back,
+        x_shared,
+        own_slot,
         stencil_table(),
         weights,
         number_k,
@@ -163,18 +192,44 @@
     drag_coeff,
     tke_coeff,
     cutoffs,
-    x_forward,
-    y_forward,
-    m_forward,
-    k_forward,
-    k_back,
-    m_back,
-    y_back,
-    x_back,
-    stencil,
-    weights,
-    number_k,
-    number_m,
+    *rest,
+):
+    table_sources, rest = rest[:TABLES], rest[TABLES:]
+    tables, rest = rest[4 : 4 + TABLES], rest[:4] + rest[4 + TABLES :]
+    step_body(
+        wind_east,
+        wind_north,
+        theta_pert,
+        tke_field,
+        target_east,
+        target_north,
+        target_theta,
+        turbine_count,
+        turbine_type,
+        drag_coeff,
+        tke_coeff,
+        cutoffs,
+        table_sources,
+        tables,
+        *rest,
+    )
+
+
+def step_body(
+    wind_east,
+    wind_north,
+    theta_pert,
+    tke_field,
+    target_east,
+    target_north,
+    target_theta,
+    turbine_count,
+    turbine_type,
+    drag_coeff,
+    tke_coeff,
+    cutoffs,
+    table_sources,
+    tables,
     east_out,
     north_out,
     theta_out,
@@ -205,7 +260,11 @@
     s4,
     r4,
     modes,
+    outer_modes,
+    operand,
+    y_first,
     in_sem,
+    table_sem,
     out_sem,
     xs_sem,
     xr_sem,
@@ -220,6 +279,22 @@
     s4_sem,
     r4_sem,
 ):
+    (
+        x_forward,
+        y_forward,
+        m_forward,
+        k_forward,
+        k_back,
+        m_back,
+        y_back,
+        x_back,
+        x_shared,
+        own_slot,
+        stencil,
+        weights,
+        number_k,
+        number_m,
+    ) = tables
     band = lax.axis_index("band")
     tile = lax.axis_index("tile")
 
@@ -233,7 +308,11 @@
         pltpu.make_async_copy(source, into, in_sem.at[i])
         for i, (source, into) in enumerate(inputs)
     ]
-    for copy in inputs:
+    table_copies = [
+        pltpu.make_async_copy(source, into, table_sem.at[i])
+        for i, (source, into) in enumerate(zip(table_sources, tables))
+    ]
+    for copy in inputs[:6] + table_copies + inputs[6:]:
         copy.start()
 
     @pl.when(tile == 0)
@@ -266,14 +345,18 @@
     low_lane = lax.rem(lane, 6) < 3
 
 
-    def pack_edges(turn, group, slot, plane):
-        xs[turn, 0, group, slot, 0:3, :] = plane[0:3]
-        xs[turn, 1, group, slot, 0:3, :] = plane[NX - 3 : NX]
-        first = slot * 6
-        mine = jnp.logical_and(lane >= first, lane < first + 6)
-        moved = pltpu.roll(plane, first + 3, 1)
-        before = jnp.where(slot == 0, jnp.zeros((NX, 128), F32), ys[turn, group])
-        ys[turn, group] = jnp.where(mine, moved, before)
+    def pack_edges(turn, group, plane_of):
+        packed = jnp.zeros((NX, 128), F32)
+        for slot in range(SLOTS):
+            plane = plane_of((slot // GLEV) * LEV + group * GLEV + slot % GLEV)
+            xs[turn, 0, group, slot, 0:3, :] = plane[0:3]
+            xs[turn, 1, group, slot, 0:3, :] = plane[NX - 3 : NX]
+            mine = jnp.logical_and(lane >= slot * 6, lane < slot * 6 + 6)
+            packed = jnp.where(mine, pltpu.roll(plane, slot * 6 + 3, 1), packed)
+        ys[turn, group] = packed
+
+    def interior(source):
+        return lambda plane: source[plane, PAD : PAD + NX, :]
 
     def x_copy(turn, group, side):
         return pltpu.make_async_remote_copy(
@@ -322,7 +405,15 @@
             def _():
                 y_copy(turn, group, 1 - side).wait_recv()
 
-        y_halo[...] = jnp.where(low_lane, yr[turn, 0, group], yr[turn, 1, group])
+    def merged_halo(turn, group):
+        return jnp.where(low_lane, yr[turn, 0, group], yr[turn, 1, group])
+
+    def fill_pads(turn, group, source):
+        for f in range(FIELDS):
+            for inner in range(GLEV):
+                plane, slot = f * LEV + group * GLEV + inner, f * GLEV + inner
+                source[plane, PAD - 3 : PAD, :] = xr[turn, 0, group, slot, 0:3, :]
+                source[plane, PAD + NX : PAD + NX + 3, :] = xr[turn, 1, group, slot, 0:3, :]
 
     def edges_sent(turn, group):
         for side in range(2):
@@ -336,20 +427,21 @@
                 y_copy(turn, group, side).wait_send()
 
 
-    def advance(turn, group, source, finish):
+    def advance(group, source, finish):
+        halo = y_halo[...]
+        for slot in range(SLOTS):
+            plane = (slot // GLEV) * LEV + group * GLEV + slot % GLEV
+            high, low = split(source[plane, PAD : PAD + NX, :])
+            halo_high, halo_low = split(pltpu.roll(halo, 128 - slot * 6, 1) if slot else halo)
+            operand[slot * NX : (slot + 1) * NX, :] = jnp.concatenate(
+                [high, low, halo_high, halo_low], axis=1
+            )
+
+        diffs[...] = dot(operand[...], stencil[...])
+
         @pl.loop(0, GLEV)
         def _(inner):
             level = group * GLEV + inner
-            rows = []
-            for f in range(FIELDS):
-                slot = f * GLEV + inner
-                plane = f * LEV + level
-                source[plane, PAD - 3 : PAD, :] = xr[turn, 0, group, slot, 0:3, :]
-                source[plane, PAD + NX : PAD + NX + 3, :] = xr[turn, 1, group, slot, 0:3, :]
-                high, low = split(source[plane, PAD : PAD + NX, :])
-                halo_high, halo_low = split(pltpu.roll(y_halo[...], 128 - slot * 6, 1))
-                rows.append(jnp.concatenate([high, low, halo_high, halo_low], axis=1))
-            diffs[...] = dot(jnp.concatenate(rows, axis=0), stencil[...])
             chunk = 16
             for at in range(0, NX, chunk):
                 east = source[level, PAD + at : PAD + at + chunk, :] * (1.0 / 60.0)
@@ -371,12 +463,13 @@
                         + 15.0 * (up1 + down1)
                         - 20.0 * cell(0)
                     )
-                    central_y = diffs[f * NX + at : f * NX + at + chunk, 0:NY]
-                    smooth_y = diffs[f * NX + at : f * NX + at + chunk, NY : 2 * NY]
+                    first = pl.multiple_of((f * GLEV + inner) * NX + at, 8)
+                    central_y = diffs[pl.ds(first, chunk), 0:NY]
+                    smooth_y = diffs[pl.ds(first, chunk), NY : 2 * NY]
                     value = (east_size * smooth - east * central) + (
                         north_size * smooth_y - north * central_y
                     )
-                    finish(f, level, plane, at, chunk, value)
+                    finish(f, plane, at, chunk, value)
 
 
     def turbines(group):
@@ -410,13 +503,9 @@
 
     @pl.loop(0, GROUPS)
     def _(group):
-        @pl.loop(0, GLEV)
-        def _(inner):
-            for f in range(FIELDS):
-                plane = f * LEV + group * GLEV + inner
-                pack_edges(0, group, f * GLEV + inner, q0[plane, PAD : PAD + NX, :])
-
-    for copy in inputs[3:6]:
+        pack_edges(0, group, interior(q0))
+
+    for copy in inputs[3:6] + table_copies:
         copy.wait()
 
     @pl.loop(0, BANDS)
@@ -486,7 +575,7 @@
     for copy in inputs[6:]:
         copy.wait()
 
-    def first_finish(f, level, plane, at, chunk, value):
+    def first_finish(f, plane, at, chunk, value):
         if f < 2:
             value = value + drag[plane, at : at + chunk, :]
         partial[plane, at : at + chunk, :] = value
@@ -495,7 +584,13 @@
         turbines(group)
         tke_copy(group).start()
         await_edges(0, group)
-        advance(0, group, q0, first_finish)
+        fill_pads(0, group, q0)
+        halo = merged_halo(0, group)
+        y_first[group] = halo
+        y_halo[...] = halo
+        advance(group, q0, first_finish)
+        pack_edges(1, group, lambda plane: partial[plane])
+        send_edges(1, group)
 
     first_stage(0)
     receive_all(*phase1)
@@ -562,48 +657,57 @@
     for half in range(2):
         columns = r4[4 * half : 4 * half + 4].reshape(4 * RY, 128).T
         wide = dot(jnp.concatenate(split(columns), axis=0), y_back[...])
-        wide = quarters(wide, 128, 4 * NY)
+        wide = quarters(wide, 128, 8 * NY)
         for i in range(4):
             modes[4 * half + i] = wide[:, i * NY : (i + 1) * NY]
+            outer_modes[4 * half + i] = wide[:, (4 + i) * NY : (5 + i) * NY] * own_slot[i % 2]
+
+    third = 1.0 / 3.0
+    inside_x = [jnp.where(flag[0], 1.0, 0.0) for flag in has]
+    inside_y = jnp.where(
+        low_lane, jnp.where(has[0][1], 1.0, 0.0), jnp.where(has[1][1], 1.0, 0.0)
+    )
+
+    def second_finish(f, plane, at, chunk, value):
+        q2[plane, PAD + at : PAD + at + chunk, :] = q0[
+            plane, PAD + at : PAD + at + chunk, :
+        ] + 0.5 * (value + force[plane, at : at + chunk, :])
 
     @pl.loop(0, GROUPS)
     def _(group):
+        await_edges(1, group)
+        outer = jnp.zeros((NX, 128), F32)
         for pair in range(2):
             high, low = split(modes[2 * group + pair])
             smooth_part = dot(x_back[...], jnp.concatenate([high, low, high], axis=0))
+            high, low = split(outer_modes[2 * group + pair])
+            outer = outer + dot(x_shared[...], jnp.concatenate([high, low, high], axis=0))
             for f in range(FIELDS):
                 for inner in range(2):
                     plane = f * LEV + group * GLEV + 2 * pair + inner
-                    at = (2 * f + inner) * NX
-                    nudge = smooth_part[at : at + NX]
+                    slot = f * GLEV + 2 * pair + inner
+                    p = 2 * f + inner
+                    nudge = smooth_part[p * NX : (p + 1) * NX]
                     if f < 2:
                         force[plane] = nudge + drag[plane]
                     else:
                         force[plane] = nudge
-                    value = q0[plane, PAD : PAD + NX, :] + (1.0 / 3.0) * (nudge + partial[plane])
-                    q1[plane, PAD : PAD + NX, :] = value
-                    pack_edges(1, group, f * GLEV + 2 * pair + inner, value)
-        send_edges(1, group)
-
-    def second_finish(f, level, plane, at, chunk, value):
-        q2[plane, PAD + at : PAD + at + chunk, :] = q0[
-            plane, PAD + at : PAD + at + chunk, :
-        ] + 0.5 * (value + force[plane, at : at + chunk, :])
-
-    @pl.loop(0, GROUPS)
-    def _(group):
-        await_edges(1, group)
-        advance(1, group, q1, second_finish)
-
-        @pl.loop(0, GLEV)
-        def _(inner):
-            for f in range(FIELDS):
-                plane = f * LEV + group * GLEV + inner
-                pack_edges(2, group, f * GLEV + inner, q2[plane, PAD : PAD + NX, :])
-
+                    q1[plane, PAD : PAD + NX, :] = q0[plane, PAD : PAD + NX, :] + third * (
+                        nudge + partial[plane]
+                    )
+                    for side, into in ((0, PAD - 3), (1, PAD + NX)):
+                        first = PLANES * NX + 8 * p + 4 * side
+                        q1[plane, into : into + 3, :] = xr[0, side, group, slot, 0:3, :] + third * (
+                            smooth_part[first : first + 3] * inside_x[side]
+                            + xr[1, side, group, slot, 0:3, :]
+                        )
+        y_halo[...] = y_first[group] + third * (outer * inside_y + merged_halo(1, group))
+
+        advance(group, q1, second_finish)
+        pack_edges(2, group, interior(q2))
         send_edges(2, group)
 
-    def third_finish(f, level, plane, at, chunk, value):
+    def third_finish(f, plane, at, chunk, value):
         result[plane, at : at + chunk, :] = q0[plane, PAD + at : PAD + at + chunk, :] + (
             value + force[plane, at : at + chunk, :]
         )
@@ -618,7 +722,9 @@
     @pl.loop(0, GROUPS)
     def _(group):
         await_edges(2, group)
-        advance(2, group, q2, third_finish)
+        fill_pads(2, group, q2)
+        y_halo[...] = merged_halo(2, group)
+        advance(group, q2, third_finish)
         for f in range(FIELDS):
             out_copy(f, group).start()
 
@@ -639,16 +745,16 @@
     field = jax.ShapeDtypeStruct((LEV, NX, NY), F32)
     anywhere = pl.BlockSpec(memory_space=pl.ANY)
     smem = pl.BlockSpec(memory_space=pltpu.SMEM)
-    vmem = pl.BlockSpec(memory_space=pltpu.VMEM)
     padded = pltpu.VMEM((FIELDS * LEV, NX + 2 * PAD, NY), F32)
     planes = pltpu.VMEM((FIELDS * LEV, NX, NY), F32)
     dma = pltpu.SemaphoreType.DMA
     return pl.pallas_call(
         kernel,
         out_shape=(field,) * 4,
-        in_specs=[anywhere] * 9 + [smem] * 3 + [vmem] * len(tables),
+        in_specs=[anywhere] * 9 + [smem] * 3 + [anywhere] * TABLES,
         out_specs=(anywhere,) * 4,
-        scratch_shapes=[
+        scratch_shapes=[pltpu.VMEM(table.shape, table.dtype) for table in tables]
+        + [
             padded,
             padded,
             padded,
@@ -660,7 +766,7 @@
             pltpu.VMEM((2 * LEV, NX, NY), F32),
             planes,
             planes,
-            pltpu.VMEM((FIELDS * NX, 2 * NY), F32),
+            pltpu.VMEM((SLOTS * NX, 2 * NY), F32),
             pltpu.VMEM((NX, 128), F32),
             pltpu.VMEM((3, 2, GROUPS, SLOTS, 4, 128), F32),
             pltpu.VMEM((3, 2, GROUPS, SLOTS, 4, 128), F32),
@@ -675,7 +781,11 @@
             pltpu.VMEM((BANDS, RY, 128), F32),
             pltpu.VMEM((BANDS, RY, 128), F32),
             pltpu.VMEM((BANDS, 128, NY), F32),
+            pltpu.VMEM((BANDS, 128, NY), F32),
+            pltpu.VMEM((SLOTS * NX, 4 * NY), BF),
+            pltpu.VMEM((GROUPS, NX, 128), F32),
             dma((9,)),
+            dma((TABLES,)),
             dma((4, GROUPS)),
             dma((3, 2, GROUPS)),
             dma((3, 2, GROUPS)),
@@ -691,7 +801,7 @@
             dma((BANDS,)),
         ],
         compiler_params=pltpu.CompilerParams(
-            collective_id=0, has_side_effects=True, vmem_limit_bytes=40 * 1024 * 1024
+            collective_id=0, has_side_effects=True, vmem_limit_bytes=61 * 1024 * 1024
         ),
         cost_estimate=pl.CostEstimate(
             flops=10**9, bytes_accessed=6 * 2**20, transcendentals=LEV * NX * NY

time: 74.7 us -> 50.6 us (0.68)
  local copies, waits for them, and re-layouts: 24.6 us -> 5.2 us
  Pallas kernels: 48.4 us -> 44.1 us
    unnamed x52 -> x10, local copies, waits for them, and re-layouts: 24.6 us -> 5.2 us
    pallas_call x1, Pallas kernels: 48.4 us -> 44.1 us  [shards(): pl.pallas_call(kernel, out_shape=(field,) * 4, in_specs=[anywhere] * 9 +...]
where the time goes in v1:
time: 50.6 us; the launch traced here: 49.9 us
  Pallas kernels  44.1 us (87%)
  local copies, waits for them, and re-layouts  5.2 us (10%)
  between operations  0.66 us (1%)
    pallas_call x1, Pallas kernels, shards(): pl.pallas_call(kernel, out_shape=(field,) * 4, in_specs=[anywhere] * 9 +...  44.1 us
    unnamed x10, local copies, waits for them, and re-layouts  5.2 us

profile of v1, /device:TPU:2, one launch (start us, length us, event | category | flops | bytes accessed | tf_op | source)
XLA Modules:
  0.0 49.9 jit_solution(14538734830622761465)
XLA Ops:
  0.6 44.1 %step.1 = (f32[16,64,128]{2,1,0:T(8,128)}, f32[16,64,128]{2,1,0:T(8,128)}, f32[16,64,128]{2,1,0:T(8,128)}, f32[16,64,128]{2,1,0:T(8,128)}) custom-call(f32[16,64,128]{2,1,0:T(8,128)} %wind_east.1, f32[16,64,128]{2,1,0:T(8,128)} %wind_north.1, f32[16,64,128]{2,1,0:T(8,128)} %theta_pert.1, f32[16,64,128]{2,1,0:T(8,128)} %tke_field.1, ...), custom_call_target="tpu_custom_call" | custom-call | flops 1000000000 | bytes 6291456 | tf_op jit(solution)/shard_map/step/pallas_call | solution.py:751
  44.7 0.0 copy-start.2
  44.7 1.9 %copy.34 = f32[16,64,128]{2,1,0:T(8,128)} copy(f32[16,64,128]{2,1,0:T(8,128)} %get-tuple-element.8) | data formatting | bytes 1048576
  46.7 0.0 copy-done.2
  46.7 0.0 copy-start.1
  46.7 0.8 %copy.35 = f32[16,64,128]{2,1,0:T(8,128)} copy(f32[16,64,128]{2,1,0:T(8,128)S(1)} %copy-done.2) | data formatting | bytes 1048576
  47.4 0.4 copy-done.1
  47.9 0.0 copy-start
  47.9 0.8 %copy.36 = f32[16,64,128]{2,1,0:T(8,128)} copy(f32[16,64,128]{2,1,0:T(8,128)S(1)} %copy-done.1) | data formatting | bytes 1048576
  48.7 0.4 copy-done
  49.1 0.8 %copy.37 = f32[16,64,128]{2,1,0:T(8,128)} copy(f32[16,64,128]{2,1,0:T(8,128)S(1)} %copy-done) | data formatting | bytes 1048576
Async XLA Ops:
  44.7 2.0 %copy-start.2 = (f32[16,64,128]{2,1,0:T(8,128)S(1)}, f32[16,64,128]{2,1,0:T(8,128)}, u32[]{:S(2)}) copy-start(f32[16,64,128]{2,1,0:T(8,128)} %get-tuple-element.9) | copy-start | bytes 1572868
  46.7 1.2 %copy-start.1 = (f32[16,64,128]{2,1,0:T(8,128)S(1)}, f32[16,64,128]{2,1,0:T(8,128)}, u32[]{:S(2)}) copy-start(f32[16,64,128]{2,1,0:T(8,128)} %get-tuple-element.10) | copy-start | bytes 1572868
  47.9 1.2 %copy-start = (f32[16,64,128]{2,1,0:T(8,128)S(1)}, f32[16,64,128]{2,1,0:T(8,128)}, u32[]{:S(2)}) copy-start(f32[16,64,128]{2,1,0:T(8,128)} %get-tuple-element.11) | copy-start | bytes 1572868

commit v2 on v1

--- a/solution.py
+++ b/solution.py
@@ -430,19 +430,20 @@
     def advance(group, source, finish):
         halo = y_halo[...]
         for slot in range(SLOTS):
+            place = (slot % GLEV) * FIELDS + slot // GLEV
             plane = (slot // GLEV) * LEV + group * GLEV + slot % GLEV
             high, low = split(source[plane, PAD : PAD + NX, :])
             halo_high, halo_low = split(pltpu.roll(halo, 128 - slot * 6, 1) if slot else halo)
-            operand[slot * NX : (slot + 1) * NX, :] = jnp.concatenate(
+            operand[place * NX : (place + 1) * NX, :] = jnp.concatenate(
                 [high, low, halo_high, halo_low], axis=1
             )
 
-        diffs[...] = dot(operand[...], stencil[...])
-
-        @pl.loop(0, GLEV)
-        def _(inner):
+
+        for inner in range(GLEV):
             level = group * GLEV + inner
             chunk = 16
+            own = pl.ds(inner * FIELDS * NX, FIELDS * NX)
+            diffs[own, :] = dot(operand[own, :], stencil[...])
             for at in range(0, NX, chunk):
                 east = source[level, PAD + at : PAD + at + chunk, :] * (1.0 / 60.0)
                 north = source[LEV + level, PAD + at : PAD + at + chunk, :] * (1.0 / 60.0)
@@ -463,7 +464,7 @@
                         + 15.0 * (up1 + down1)
                         - 20.0 * cell(0)
                     )
-                    first = pl.multiple_of((f * GLEV + inner) * NX + at, 8)
+                    first = (inner * FIELDS + f) * NX + at
                     central_y = diffs[pl.ds(first, chunk), 0:NY]
                     smooth_y = diffs[pl.ds(first, chunk), NY : 2 * NY]
                     value = (east_size * smooth - east * central) + (
@@ -531,28 +532,33 @@
     def _(group):
         send_edges(0, group)
 
-    def exchange(axis, count, me, source, into, send_sem, recv_sem, step):
-        other = lax.rem(me + step, count)
-        return (
-            other,
-            pltpu.make_async_remote_copy(
-                src_ref=source.at[other],
-                dst_ref=into.at[me],
-                send_sem=send_sem.at[other],
-                recv_sem=recv_sem.at[me],
-                device_id={axis: other},
-                device_id_type=MESH,
-            ),
-        )
-
-    def send_all(axis, count, me, source, into, send_sem, recv_sem):
-        for step in range(1, count):
-            exchange(axis, count, me, source, into, send_sem, recv_sem, step)[1].start()
+    def partners(axis):
+        if axis == "band":
+            return [lax.rem(band + step, BANDS) for step in (4, 3, 5, 2, 6, 1, 7)]
+        apart = sorted(
+            ((dx, dz) for dx in range(4) for dz in range(4) if dx or dz),
+            key=lambda at: -(min(at[0], 4 - at[0]) + min(at[1], 4 - at[1])),
+        )
+        x, z = tile // 4, lax.rem(tile, 4)
+        return [lax.rem(x + dx, 4) * 4 + lax.rem(z + dz, 4) for dx, dz in apart]
+
+    def outgoing(axis, me, source, into, send_sem, recv_sem, other):
+        return pltpu.make_async_remote_copy(
+            src_ref=source.at[other],
+            dst_ref=into.at[me],
+            send_sem=send_sem.at[other],
+            recv_sem=recv_sem.at[me],
+            device_id={axis: other},
+            device_id_type=MESH,
+        )
+
+    def send_all(axis, me, source, into, send_sem, recv_sem):
+        for other in partners(axis):
+            outgoing(axis, me, source, into, send_sem, recv_sem, other).start()
         into[me] = source[me]
 
-    def receive_all(axis, count, me, source, into, send_sem, recv_sem):
-        for step in range(1, count):
-            other = lax.rem(me + step, count)
+    def receive_all(axis, me, source, into, send_sem, recv_sem):
+        for other in partners(axis)[::-1]:
             pltpu.make_async_remote_copy(
                 src_ref=source.at[other],
                 dst_ref=into.at[other],
@@ -562,14 +568,14 @@
                 device_id_type=MESH,
             ).wait_recv()
 
-    def sent_all(axis, count, me, source, into, send_sem, recv_sem):
-        for step in range(1, count):
-            exchange(axis, count, me, source, into, send_sem, recv_sem, step)[1].wait_send()
-
-    phase1 = ("band", BANDS, band, s1, r1, s1_sem, r1_sem)
-    phase2 = ("tile", TILES, tile, s2, r2, s2_sem, r2_sem)
-    phase3 = ("tile", TILES, tile, s3, r3, s3_sem, r3_sem)
-    phase4 = ("band", BANDS, band, s4, r4, s4_sem, r4_sem)
+    def sent_all(axis, me, source, into, send_sem, recv_sem):
+        for other in partners(axis):
+            outgoing(axis, me, source, into, send_sem, recv_sem, other).wait_send()
+
+    phase1 = ("band", band, s1, r1, s1_sem, r1_sem)
+    phase2 = ("tile", tile, s2, r2, s2_sem, r2_sem)
+    phase3 = ("tile", tile, s3, r3, s3_sem, r3_sem)
+    phase4 = ("band", band, s4, r4, s4_sem, r4_sem)
 
     send_all(*phase1)
     for copy in inputs[6:]:
@@ -740,6 +746,30 @@
         tke_copy(group).wait()
 
 
+PARTS = 4
+
+
+def deliver(*refs):
+    sources, results, held, in_sems, out_sems = refs[:4], refs[4:8], refs[8], refs[9], refs[10]
+    inward, outward = [], []
+    for j in range(PARTS):
+        rows = pl.ds(j * (LEV // PARTS), LEV // PARTS)
+        for i in range(4):
+            inward.append(
+                pltpu.make_async_copy(sources[i].at[rows], held.at[i, rows], in_sems.at[i, j])
+            )
+            outward.append(
+                pltpu.make_async_copy(held.at[i, rows], results[i].at[rows], out_sems.at[i, j])
+            )
+    for copy in inward:
+        copy.start()
+    for first, second in zip(inward, outward):
+        first.wait()
+        second.start()
+    for copy in outward:
+        copy.wait()
+
+
 def shards(*arguments):
     tables = [jnp.asarray(table) for table in make_tables()]
     field = jax.ShapeDtypeStruct((LEV, NX, NY), F32)
@@ -748,7 +778,7 @@
     padded = pltpu.VMEM((FIELDS * LEV, NX + 2 * PAD, NY), F32)
     planes = pltpu.VMEM((FIELDS * LEV, NX, NY), F32)
     dma = pltpu.SemaphoreType.DMA
-    return pl.pallas_call(
+    outcome = pl.pallas_call(
         kernel,
         out_shape=(field,) * 4,
         in_specs=[anywhere] * 9 + [smem] * 3 + [anywhere] * TABLES,
@@ -808,6 +838,19 @@
         ),
         name="step",
     )(*arguments, *tables)
+    return pl.pallas_call(
+        deliver,
+        out_shape=(field,) * 4,
+        in_specs=[anywhere] * 4,
+        out_specs=(anywhere,) * 4,
+        scratch_shapes=[
+            pltpu.VMEM((4, LEV, NX, NY), F32),
+            dma((4, PARTS)),
+            dma((4, PARTS)),
+        ],
+        compiler_params=pltpu.CompilerParams(vmem_limit_bytes=61 * 1024 * 1024),
+        name="deliver",
+    )(*outcome)
 
 
 def solution(mesh):

time: 50.6 us -> 45.7 us (0.903)
  local copies, waits for them, and re-layouts: 5.2 us -> 0 us
  Pallas kernels: 44.1 us -> 44.8 us
    unnamed x10 -> x0, local copies, waits for them, and re-layouts: 5.2 us -> none
    pallas_call x0 -> x1, Pallas kernels: none -> 2.57 us  [shards(): pl.pallas_call(deliver, out_shape=(field,) * 4, in_specs=[anywhere] * 4,...]
    pallas_call x1, Pallas kernels: 44.1 us -> 42.2 us  [shards(): pl.pallas_call(kernel, out_shape=(field,) * 4, in_specs=[anywhere] * 9 +...]
where the time goes in v2:
time: 45.7 us; the launch traced here: 45.4 us
  Pallas kernels  44.8 us (98%)
  between operations  0.64 us (1%)
    pallas_call x1, Pallas kernels, shards(): pl.pallas_call(kernel, out_shape=(field,) * 4, in_specs=[anywhere] * 9 +...  42.2 us
    pallas_call x1, Pallas kernels, shards(): pl.pallas_call(deliver, out_shape=(field,) * 4, in_specs=[anywhere] * 4,...  2.57 us

profile of v2, /device:TPU:2, one launch (start us, length us, event | category | flops | bytes accessed | tf_op | source)
XLA Modules:
  0.0 45.4 jit_solution(7015955362860836185)
XLA Ops:
  0.6 42.2 %step.1 = (f32[16,64,128]{2,1,0:T(8,128)}, f32[16,64,128]{2,1,0:T(8,128)}, f32[16,64,128]{2,1,0:T(8,128)}, f32[16,64,128]{2,1,0:T(8,128)}) custom-call(f32[16,64,128]{2,1,0:T(8,128)} %wind_east.1, f32[16,64,128]{2,1,0:T(8,128)} %wind_north.1, f32[16,64,128]{2,1,0:T(8,128)} %theta_pert.1, f32[16,64,128]{2,1,0:T(8,128)} %tke_field.1, ...), custom_call_target="tpu_custom_call" | custom-call | flops 1000000000 | bytes 6291456 | tf_op jit(solution)/shard_map/step/pallas_call | solution.py:781
  42.8 2.6 %deliver.1 = (f32[16,64,128]{2,1,0:T(8,128)}, f32[16,64,128]{2,1,0:T(8,128)}, f32[16,64,128]{2,1,0:T(8,128)}, f32[16,64,128]{2,1,0:T(8,128)}) custom-call(f32[16,64,128]{2,1,0:T(8,128)} %get-tuple-element.8.refs_0_, f32[16,64,128]{2,1,0:T(8,128)} %get-tuple-element.9.refs_1_, f32[16,64,128]{2,1,0:T(8,128)} %get-tuple-element.10.refs_2_, ...), custom_call_target="tpu_custom_call" | custom-call | tf_op jit(solution)/shard_map/deliver/pallas_call | solution.py:841

commit v3 on v2

--- a/solution.py
+++ b/solution.py
@@ -111,18 +111,16 @@
     y_forward = np.concatenate(
         [np.concatenate([high, high], axis=1), np.concatenate([low, 0 * low], axis=1)], axis=0
     )
-    inner_y, outer_y = wy[3 : NY + 3].T, np.zeros((RY, NY))
-    outer_y[:, : 6 * SLOTS] = np.tile(np.concatenate([wy[:3], wy[NY + 3 :]]).T, (1, SLOTS))
-    diag = np.zeros((4 * RY, 8 * NY))
-    for g in range(4):
-        diag[g * RY : (g + 1) * RY, g * NY : (g + 1) * NY] = inner_y
-        diag[g * RY : (g + 1) * RY, (4 + g) * NY : (5 + g) * NY] = outer_y
-    y_back = np.concatenate(halves(diag), axis=1)
+    both_y = np.zeros((2 * NY, RY))
+    both_y[:NY] = wy[3 : NY + 3]
+    both_y[NY : NY + 6 * SLOTS] = np.tile(np.concatenate([wy[:3], wy[NY + 3 :]]), (SLOTS, 1))
+    high, low = halves(both_y)
+    y_back = np.concatenate([high, high, low, 0 * low], axis=1)
     own_slot = np.zeros((2, 128, 128), np.float32)
     for pair in range(2):
         for p in range(PLANES):
             slot = (p // 2) * GLEV + 2 * pair + p % 2
-            own_slot[pair, p * RX : (p + 1) * RX, 6 * slot : 6 * slot + 6] = 1
+            own_slot[pair, 6 * slot : 6 * slot + 6, p * RX : (p + 1) * RX] = 1
 
     uy_all = np.concatenate(uy, axis=1)
     m_forward = np.concatenate(halves(uy_all), axis=0)
@@ -298,21 +296,34 @@
     band = lax.axis_index("band")
     tile = lax.axis_index("tile")
 
-    inputs = []
-    for f, source in enumerate((wind_east, wind_north, theta_pert)):
-        inputs.append((source, q0.at[pl.ds(f * LEV, LEV), pl.ds(PAD, NX), :]))
-    for f, source in enumerate((target_east, target_north, target_theta)):
-        inputs.append((source, target.at[pl.ds(f * LEV, LEV)]))
-    inputs += [(tke_field, tke), (turbine_count, count), (turbine_type, kind)]
-    inputs = [
-        pltpu.make_async_copy(source, into, in_sem.at[i])
-        for i, (source, into) in enumerate(inputs)
+    def field_copies(group):
+        rows = pl.ds(group * GLEV, GLEV)
+        copies = []
+        for f, source in enumerate((wind_east, wind_north, theta_pert)):
+            into = q0.at[pl.ds(f * LEV + group * GLEV, GLEV), pl.ds(PAD, NX), :]
+            copies.append(pltpu.make_async_copy(source.at[rows], into, in_sem.at[f, group]))
+        for f, source in enumerate((target_east, target_north, target_theta)):
+            into = target.at[pl.ds(f * LEV + group * GLEV, GLEV)]
+            copies.append(pltpu.make_async_copy(source.at[rows], into, in_sem.at[3 + f, group]))
+        return copies
+
+    others = [
+        pltpu.make_async_copy(source, into, in_sem.at[6 + i, 0])
+        for i, (source, into) in enumerate(
+            ((tke_field, tke), (turbine_count, count), (turbine_type, kind))
+        )
     ]
     table_copies = [
         pltpu.make_async_copy(source, into, table_sem.at[i])
         for i, (source, into) in enumerate(zip(table_sources, tables))
     ]
-    for copy in inputs[:6] + table_copies + inputs[6:]:
+    for copy in table_copies[:2]:
+        copy.start()
+
+    for group in range(GROUPS):
+        for copy in field_copies(group):
+            copy.start()
+    for copy in others + table_copies[2:]:
         copy.start()
 
     @pl.when(tile == 0)
@@ -499,18 +510,10 @@
         return pltpu.make_async_copy(tke.at[rows], tke_out.at[rows], out_sem.at[3, group])
 
 
-    for copy in inputs[:3]:
+    for copy in table_copies[:2]:
         copy.wait()
 
-    @pl.loop(0, GROUPS)
-    def _(group):
-        pack_edges(0, group, interior(q0))
-
-    for copy in inputs[3:6] + table_copies:
-        copy.wait()
-
-    @pl.loop(0, BANDS)
-    def _(to):
+    def coefficients(to):
         rows = []
         for f in range(FIELDS):
             part = pl.ds(f * LEV + 2 * to, 2)
@@ -526,11 +529,14 @@
         )
         s1[to] = both[:RY] + both[RY:]
 
-    pl.semaphore_wait(barrier, BANDS - 1 + TILES - 1)
-
     @pl.loop(0, GROUPS)
     def _(group):
-        send_edges(0, group)
+        for copy in field_copies(group):
+            copy.wait()
+        for pair in range(2):
+            coefficients(2 * group + pair)
+
+    pl.semaphore_wait(barrier, BANDS - 1 + TILES - 1)
 
     def partners(axis):
         if axis == "band":
@@ -578,8 +584,19 @@
     phase4 = ("band", band, s4, r4, s4_sem, r4_sem)
 
     send_all(*phase1)
-    for copy in inputs[6:]:
+
+    @pl.loop(0, GROUPS)
+    def _(group):
+        pack_edges(0, group, interior(q0))
+        send_edges(0, group)
+
+    for copy in others + table_copies[2:]:
         copy.wait()
+
+    @pl.loop(0, GROUPS)
+    def _(group):
+        turbines(group)
+        tke_copy(group).start()
 
     def first_finish(f, plane, at, chunk, value):
         if f < 2:
@@ -587,8 +604,6 @@
         partial[plane, at : at + chunk, :] = value
 
     def first_stage(group):
-        turbines(group)
-        tke_copy(group).start()
         await_edges(0, group)
         fill_pads(0, group, q0)
         halo = merged_halo(0, group)
@@ -598,14 +613,17 @@
         pack_edges(1, group, lambda plane: partial[plane])
         send_edges(1, group)
 
-    first_stage(0)
     receive_all(*phase1)
 
     received = r1[...].reshape(BANDS * RY, 128)
     columns = jnp.concatenate(split(received), axis=1)
     s2[...] = quarters(dot(m_forward[...], columns), MODES, 128).reshape(TILES, 8, 128)
     send_all(*phase2)
-    first_stage(1)
+
+    @pl.loop(0, 2)
+    def _(group):
+        first_stage(group)
+
     receive_all(*phase2)
 
     lane8 = lax.broadcasted_iota(jnp.int32, (8, 128), 1)
@@ -650,23 +668,41 @@
             value = jnp.where(inside[p], moved, value)
         s3[t] = value
     send_all(*phase3)
-    first_stage(2)
+
+    @pl.loop(2, 4)
+    def _(group):
+        first_stage(group)
+
     receive_all(*phase3)
 
     received = r3[...].reshape(MODES, 128)
     back = quarters(dot(m_back[...], jnp.concatenate(split(received), axis=1)), BANDS * RY, 128)
     s4[...] = back.reshape(BANDS, RY, 128)
     send_all(*phase4)
-    first_stage(3)
     receive_all(*phase4)
 
-    for half in range(2):
-        columns = r4[4 * half : 4 * half + 4].reshape(4 * RY, 128).T
-        wide = dot(jnp.concatenate(split(columns), axis=0), y_back[...])
-        wide = quarters(wide, 128, 8 * NY)
-        for i in range(4):
-            modes[4 * half + i] = wide[:, i * NY : (i + 1) * NY]
-            outer_modes[4 * half + i] = wide[:, (4 + i) * NY : (5 + i) * NY] * own_slot[i % 2]
+    columns = []
+    for of in range(BANDS):
+        high, low = split(r4[of])
+        columns.append(jnp.concatenate([high, low, high, jnp.zeros((RY, 128), BF)], axis=0))
+    wide = dot(y_back[...], jnp.concatenate(columns, axis=1))
+    for of in range(BANDS):
+        modes[of] = wide[:NY, of * 128 : (of + 1) * 128]
+    for group in range(GROUPS):
+        first = 2 * group * 128
+        outer_modes[group] = (
+            wide[NY:, first : first + 128] * own_slot[0]
+            + wide[NY:, first + 128 : first + 256] * own_slot[1]
+        )
+
+    def across(table, value):
+        high, low = split(value)
+        return lax.dot_general(
+            table,
+            jnp.concatenate([high, low, high], axis=1),
+            (((1,), (1,)), ((), ())),
+            preferred_element_type=F32,
+        )
 
     third = 1.0 / 3.0
     inside_x = [jnp.where(flag[0], 1.0, 0.0) for flag in has]
@@ -682,12 +718,11 @@
     @pl.loop(0, GROUPS)
     def _(group):
         await_edges(1, group)
-        outer = jnp.zeros((NX, 128), F32)
+        outer = across(x_shared[...], outer_modes[group])
+        pairs = modes[pl.ds(2 * group, 2)].reshape(2 * NY, 128)
+        smooth_pairs = across(x_back[...], pairs)
         for pair in range(2):
-            high, low = split(modes[2 * group + pair])
-            smooth_part = dot(x_back[...], jnp.concatenate([high, low, high], axis=0))
-            high, low = split(outer_modes[2 * group + pair])
-            outer = outer + dot(x_shared[...], jnp.concatenate([high, low, high], axis=0))
+            smooth_part = smooth_pairs[:, pair * NY : (pair + 1) * NY]
             for f in range(FIELDS):
                 for inner in range(2):
                     plane = f * LEV + group * GLEV + 2 * pair + inner
@@ -746,7 +781,7 @@
         tke_copy(group).wait()
 
 
-PARTS = 4
+PARTS = 2
 
 
 def deliver(*refs):
@@ -810,11 +845,11 @@
             pltpu.VMEM((TILES, 8, 128), F32),
             pltpu.VMEM((BANDS, RY, 128), F32),
             pltpu.VMEM((BANDS, RY, 128), F32),
-            pltpu.VMEM((BANDS, 128, NY), F32),
-            pltpu.VMEM((BANDS, 128, NY), F32),
+            pltpu.VMEM((BANDS, NY, 128), F32),
+            pltpu.VMEM((GROUPS, NY, 128), F32),
             pltpu.VMEM((SLOTS * NX, 4 * NY), BF),
             pltpu.VMEM((GROUPS, NX, 128), F32),
-            dma((9,)),
+            dma((9, GROUPS)),
             dma((TABLES,)),
             dma((4, GROUPS)),
             dma((3, 2, GROUPS)),

time: 45.7 us -> 43.2 us (0.945)
  Pallas kernels: 44.8 us -> 42.3 us
    pallas_call x1, Pallas kernels: 42.2 us -> 39.9 us  [shards(): pl.pallas_call(kernel, out_shape=(field,) * 4, in_specs=[anywhere] * 9 +...]
where the time goes in v3:
time: 43.2 us; the launch traced here: 43 us
  Pallas kernels  42.3 us (98%)
  between operations  0.64 us (1%)
    pallas_call x1, Pallas kernels, shards(): pl.pallas_call(kernel, out_shape=(field,) * 4, in_specs=[anywhere] * 9 +...  39.9 us
    pallas_call x1, Pallas kernels, shards(): pl.pallas_call(deliver, out_shape=(field,) * 4, in_specs=[anywhere] * 4,...  2.4 us

profile of v3, /device:TPU:2, one launch (start us, length us, event | category | flops | bytes accessed | tf_op | source)
XLA Modules:
  0.0 43.0 jit_solution(5527691623178541803)
XLA Ops:
  0.6 39.9 %step.1 = (f32[16,64,128]{2,1,0:T(8,128)}, f32[16,64,128]{2,1,0:T(8,128)}, f32[16,64,128]{2,1,0:T(8,128)}, f32[16,64,128]{2,1,0:T(8,128)}) custom-call(f32[16,64,128]{2,1,0:T(8,128)} %wind_east.1, f32[16,64,128]{2,1,0:T(8,128)} %wind_north.1, f32[16,64,128]{2,1,0:T(8,128)} %theta_pert.1, f32[16,64,128]{2,1,0:T(8,128)} %tke_field.1, ...), custom_call_target="tpu_custom_call" | custom-call | flops 1000000000 | bytes 6291456 | tf_op jit(solution)/shard_map/step/pallas_call | solution.py:816
  40.6 2.4 %deliver.1 = (f32[16,64,128]{2,1,0:T(8,128)}, f32[16,64,128]{2,1,0:T(8,128)}, f32[16,64,128]{2,1,0:T(8,128)}, f32[16,64,128]{2,1,0:T(8,128)}) custom-call(f32[16,64,128]{2,1,0:T(8,128)} %get-tuple-element.8.refs_0_, f32[16,64,128]{2,1,0:T(8,128)} %get-tuple-element.9.refs_1_, f32[16,64,128]{2,1,0:T(8,128)} %get-tuple-element.10.refs_2_, ...), custom_call_target="tpu_custom_call" | custom-call | tf_op jit(solution)/shard_map/deliver/pallas_call | solution.py:876

commit v4 on v3

--- a/solution.py
+++ b/solution.py
@@ -260,7 +260,6 @@
     modes,
     outer_modes,
     operand,
-    y_first,
     in_sem,
     table_sem,
     out_sem,
@@ -343,13 +342,13 @@
         yr[:, 1] = jnp.zeros((3, GROUPS, NX, 128), F32)
 
     barrier = pltpu.get_barrier_semaphore()
+    for step in range(1, TILES):
+        pl.semaphore_signal(
+            barrier, inc=1, device_id={"tile": lax.rem(tile + step, TILES)}, device_id_type=MESH
+        )
     for step in range(1, BANDS):
         pl.semaphore_signal(
             barrier, inc=1, device_id={"band": lax.rem(band + step, BANDS)}, device_id_type=MESH
-        )
-    for step in range(1, TILES):
-        pl.semaphore_signal(
-            barrier, inc=1, device_id={"tile": lax.rem(tile + step, TILES)}, device_id_type=MESH
         )
 
     lane = lax.broadcasted_iota(jnp.int32, (NX, 128), 1)
@@ -598,17 +597,19 @@
         turbines(group)
         tke_copy(group).start()
 
+    third = 1.0 / 3.0
+
     def first_finish(f, plane, at, chunk, value):
         if f < 2:
             value = value + drag[plane, at : at + chunk, :]
-        partial[plane, at : at + chunk, :] = value
+        partial[plane, at : at + chunk, :] = (
+            q0[plane, PAD + at : PAD + at + chunk, :] + third * value
+        )
 
     def first_stage(group):
         await_edges(0, group)
         fill_pads(0, group, q0)
-        halo = merged_halo(0, group)
-        y_first[group] = halo
-        y_halo[...] = halo
+        y_halo[...] = merged_halo(0, group)
         advance(group, q0, first_finish)
         pack_edges(1, group, lambda plane: partial[plane])
         send_edges(1, group)
@@ -620,7 +621,7 @@
     s2[...] = quarters(dot(m_forward[...], columns), MODES, 128).reshape(TILES, 8, 128)
     send_all(*phase2)
 
-    @pl.loop(0, 2)
+    @pl.loop(0, GROUPS)
     def _(group):
         first_stage(group)
 
@@ -669,16 +670,22 @@
         s3[t] = value
     send_all(*phase3)
 
-    @pl.loop(2, 4)
-    def _(group):
-        first_stage(group)
-
     receive_all(*phase3)
 
     received = r3[...].reshape(MODES, 128)
     back = quarters(dot(m_back[...], jnp.concatenate(split(received), axis=1)), BANDS * RY, 128)
     s4[...] = back.reshape(BANDS, RY, 128)
     send_all(*phase4)
+    for phase in (phase1, phase2, phase3):
+        sent_all(*phase)
+
+    @pl.loop(0, GROUPS)
+    def _(group):
+        edges_sent(0, group)
+        edges_sent(1, group)
+        tke_copy(group).wait()
+        await_edges(1, group)
+
     receive_all(*phase4)
 
     columns = []
@@ -704,10 +711,9 @@
             preferred_element_type=F32,
         )
 
-    third = 1.0 / 3.0
-    inside_x = [jnp.where(flag[0], 1.0, 0.0) for flag in has]
+    inside_x = [jnp.where(flag[0], third, 0.0) for flag in has]
     inside_y = jnp.where(
-        low_lane, jnp.where(has[0][1], 1.0, 0.0), jnp.where(has[1][1], 1.0, 0.0)
+        low_lane, jnp.where(has[0][1], third, 0.0), jnp.where(has[1][1], third, 0.0)
     )
 
     def second_finish(f, plane, at, chunk, value):
@@ -717,7 +723,6 @@
 
     @pl.loop(0, GROUPS)
     def _(group):
-        await_edges(1, group)
         outer = across(x_shared[...], outer_modes[group])
         pairs = modes[pl.ds(2 * group, 2)].reshape(2 * NY, 128)
         smooth_pairs = across(x_back[...], pairs)
@@ -733,16 +738,13 @@
                         force[plane] = nudge + drag[plane]
                     else:
                         force[plane] = nudge
-                    q1[plane, PAD : PAD + NX, :] = q0[plane, PAD : PAD + NX, :] + third * (
-                        nudge + partial[plane]
-                    )
+                    q1[plane, PAD : PAD + NX, :] = partial[plane] + third * nudge
                     for side, into in ((0, PAD - 3), (1, PAD + NX)):
                         first = PLANES * NX + 8 * p + 4 * side
-                        q1[plane, into : into + 3, :] = xr[0, side, group, slot, 0:3, :] + third * (
-                            smooth_part[first : first + 3] * inside_x[side]
-                            + xr[1, side, group, slot, 0:3, :]
-                        )
-        y_halo[...] = y_first[group] + third * (outer * inside_y + merged_halo(1, group))
+                        q1[plane, into : into + 3, :] = xr[
+                            1, side, group, slot, 0:3, :
+                        ] + smooth_part[first : first + 3] * inside_x[side]
+        y_halo[...] = merged_halo(1, group) + outer * inside_y
 
         advance(group, q1, second_finish)
         pack_edges(2, group, interior(q2))
@@ -769,16 +771,13 @@
         for f in range(FIELDS):
             out_copy(f, group).start()
 
-    for phase in (phase1, phase2, phase3, phase4):
-        sent_all(*phase)
+    sent_all(*phase4)
 
     @pl.loop(0, GROUPS)
     def _(group):
-        for turn in range(3):
-            edges_sent(turn, group)
+        edges_sent(2, group)
         for f in range(FIELDS):
             out_copy(f, group).wait()
-        tke_copy(group).wait()
 
 
 PARTS = 2
@@ -848,7 +847,6 @@
             pltpu.VMEM((BANDS, NY, 128), F32),
             pltpu.VMEM((GROUPS, NY, 128), F32),
             pltpu.VMEM((SLOTS * NX, 4 * NY), BF),
-            pltpu.VMEM((GROUPS, NX, 128), F32),
             dma((9, GROUPS)),
             dma((TABLES,)),
             dma((4, GROUPS)),

time: 43.2 us -> 42.7 us (0.988)
  no operation moved by 1% of the time
where the time goes in v4:
time: 42.7 us; the launch traced here: 42.6 us
  Pallas kernels  41.9 us (98%)
  between operations  0.64 us (1%)
    pallas_call x1, Pallas kernels, shards(): pl.pallas_call(kernel, out_shape=(field,) * 4, in_specs=[anywhere] * 9 +...  39.5 us
    pallas_call x1, Pallas kernels, shards(): pl.pallas_call(deliver, out_shape=(field,) * 4, in_specs=[anywhere] * 4,...  2.4 us

profile of v4, /device:TPU:2, one launch (start us, length us, event | category | flops | bytes accessed | tf_op | source)
XLA Modules:
  0.0 42.6 jit_solution(7399388646494736497)
XLA Ops:
  0.6 39.5 %step.1 = (f32[16,64,128]{2,1,0:T(8,128)}, f32[16,64,128]{2,1,0:T(8,128)}, f32[16,64,128]{2,1,0:T(8,128)}, f32[16,64,128]{2,1,0:T(8,128)}) custom-call(f32[16,64,128]{2,1,0:T(8,128)} %wind_east.1, f32[16,64,128]{2,1,0:T(8,128)} %wind_north.1, f32[16,64,128]{2,1,0:T(8,128)} %theta_pert.1, f32[16,64,128]{2,1,0:T(8,128)} %tke_field.1, ...), custom_call_target="tpu_custom_call" | custom-call | flops 1000000000 | bytes 6291456 | tf_op jit(solution)/shard_map/step/pallas_call | solution.py:815
  40.2 2.4 %deliver.1 = (f32[16,64,128]{2,1,0:T(8,128)}, f32[16,64,128]{2,1,0:T(8,128)}, f32[16,64,128]{2,1,0:T(8,128)}, f32[16,64,128]{2,1,0:T(8,128)}) custom-call(f32[16,64,128]{2,1,0:T(8,128)} %get-tuple-element.8.refs_0_, f32[16,64,128]{2,1,0:T(8,128)} %get-tuple-element.9.refs_1_, f32[16,64,128]{2,1,0:T(8,128)} %get-tuple-element.10.refs_2_, ...), custom_call_target="tpu_custom_call" | custom-call | tf_op jit(solution)/shard_map/deliver/pallas_call | solution.py:874

commit v5 on v4

--- a/solution.py
+++ b/solution.py
@@ -319,7 +319,21 @@
     for copy in table_copies[:2]:
         copy.start()
 
-    for group in range(GROUPS):
+    for group in range(1):
+        for copy in field_copies(group):
+            copy.start()
+
+    barrier = pltpu.get_barrier_semaphore()
+    for step in range(1, TILES):
+        pl.semaphore_signal(
+            barrier, inc=1, device_id={"tile": lax.rem(tile + step, TILES)}, device_id_type=MESH
+        )
+    for step in range(1, BANDS):
+        pl.semaphore_signal(
+            barrier, inc=1, device_id={"band": lax.rem(band + step, BANDS)}, device_id_type=MESH
+        )
+
+    for group in range(1, GROUPS):
         for copy in field_copies(group):
             copy.start()
     for copy in others + table_copies[2:]:
@@ -340,16 +354,6 @@
     @pl.when(band == BANDS - 1)
     def _():
         yr[:, 1] = jnp.zeros((3, GROUPS, NX, 128), F32)
-
-    barrier = pltpu.get_barrier_semaphore()
-    for step in range(1, TILES):
-        pl.semaphore_signal(
-            barrier, inc=1, device_id={"tile": lax.rem(tile + step, TILES)}, device_id_type=MESH
-        )
-    for step in range(1, BANDS):
-        pl.semaphore_signal(
-            barrier, inc=1, device_id={"band": lax.rem(band + step, BANDS)}, device_id_type=MESH
-        )
 
     lane = lax.broadcasted_iota(jnp.int32, (NX, 128), 1)
     low_lane = lax.rem(lane, 6) < 3

time: 42.7 us -> 42.5 us (level)
  no operation moved by 1% of the time
where the time goes in v5:
time: 42.5 us; the launch traced here: 42.3 us
  Pallas kernels  41.7 us (98%)
  between operations  0.64 us (2%)
    pallas_call x1, Pallas kernels, shards(): pl.pallas_call(kernel, out_shape=(field,) * 4, in_specs=[anywhere] * 9 +...  39.3 us
    pallas_call x1, Pallas kernels, shards(): pl.pallas_call(deliver, out_shape=(field,) * 4, in_specs=[anywhere] * 4,...  2.4 us

profile of v5, /device:TPU:2, one launch (start us, length us, event | category | flops | bytes accessed | tf_op | source)
XLA Modules:
  0.0 42.3 jit_solution(4388259034016273992)
XLA Ops:
  0.6 39.3 %step.1 = (f32[16,64,128]{2,1,0:T(8,128)}, f32[16,64,128]{2,1,0:T(8,128)}, f32[16,64,128]{2,1,0:T(8,128)}, f32[16,64,128]{2,1,0:T(8,128)}) custom-call(f32[16,64,128]{2,1,0:T(8,128)} %wind_east.1, f32[16,64,128]{2,1,0:T(8,128)} %wind_north.1, f32[16,64,128]{2,1,0:T(8,128)} %theta_pert.1, f32[16,64,128]{2,1,0:T(8,128)} %tke_field.1, ...), custom_call_target="tpu_custom_call" | custom-call | flops 1000000000 | bytes 6291456 | tf_op jit(solution)/shard_map/step/pallas_call | solution.py:819
  39.9 2.4 %deliver.1 = (f32[16,64,128]{2,1,0:T(8,128)}, f32[16,64,128]{2,1,0:T(8,128)}, f32[16,64,128]{2,1,0:T(8,128)}, f32[16,64,128]{2,1,0:T(8,128)}) custom-call(f32[16,64,128]{2,1,0:T(8,128)} %get-tuple-element.8.refs_0_, f32[16,64,128]{2,1,0:T(8,128)} %get-tuple-element.9.refs_1_, f32[16,64,128]{2,1,0:T(8,128)} %get-tuple-element.10.refs_2_, ...), custom_call_target="tpu_custom_call" | custom-call | tf_op jit(solution)/shard_map/deliver/pallas_call | solution.py:878

commit v6 on v5

--- a/solution.py
+++ b/solution.py
@@ -455,7 +455,7 @@
 
         for inner in range(GLEV):
             level = group * GLEV + inner
-            chunk = 16
+            chunk = 32
             own = pl.ds(inner * FIELDS * NX, FIELDS * NX)
             diffs[own, :] = dot(operand[own, :], stencil[...])
             for at in range(0, NX, chunk):

time: 42.5 us -> 42.5 us (level)
  no operation moved by 1% of the time
where the time goes in v6:
time: 42.5 us; the launch traced here: 42.3 us
  Pallas kernels  41.7 us (98%)
  between operations  0.64 us (2%)
    pallas_call x1, Pallas kernels, shards(): pl.pallas_call(kernel, out_shape=(field,) * 4, in_specs=[anywhere] * 9 +...  39.3 us
    pallas_call x1, Pallas kernels, shards(): pl.pallas_call(deliver, out_shape=(field,) * 4, in_specs=[anywhere] * 4,...  2.4 us

profile of v6, /device:TPU:2, one launch (start us, length us, event | category | flops | bytes accessed | tf_op | source)
XLA Modules:
  0.0 42.3 jit_solution(1654778373059404147)
XLA Ops:
  0.6 39.3 %step.1 = (f32[16,64,128]{2,1,0:T(8,128)}, f32[16,64,128]{2,1,0:T(8,128)}, f32[16,64,128]{2,1,0:T(8,128)}, f32[16,64,128]{2,1,0:T(8,128)}) custom-call(f32[16,64,128]{2,1,0:T(8,128)} %wind_east.1, f32[16,64,128]{2,1,0:T(8,128)} %wind_north.1, f32[16,64,128]{2,1,0:T(8,128)} %theta_pert.1, f32[16,64,128]{2,1,0:T(8,128)} %tke_field.1, ...), custom_call_target="tpu_custom_call" | custom-call | flops 1000000000 | bytes 6291456 | tf_op jit(solution)/shard_map/step/pallas_call | solution.py:819
  39.9 2.4 %deliver.1 = (f32[16,64,128]{2,1,0:T(8,128)}, f32[16,64,128]{2,1,0:T(8,128)}, f32[16,64,128]{2,1,0:T(8,128)}, f32[16,64,128]{2,1,0:T(8,128)}) custom-call(f32[16,64,128]{2,1,0:T(8,128)} %get-tuple-element.8.refs_0_, f32[16,64,128]{2,1,0:T(8,128)} %get-tuple-element.9.refs_1_, f32[16,64,128]{2,1,0:T(8,128)} %get-tuple-element.10.refs_2_, ...), custom_call_target="tpu_custom_call" | custom-call | tf_op jit(solution)/shard_map/deliver/pallas_call | solution.py:878
